TPU v7x, 32 devices: a whole 2x2x4 slice. The times are simulated.
32 devices in a mesh: row: 4 (over y, x), col: 8 (over z, core).
Axes of the slice: x: 2, y: 2, z: 4, core: 2. Of those that a mesh axis runs over, the one named last changes fastest.
Arguments:
- design: bfloat16 [2048, 24576], P('row', 'col'), may hold values from -0.125 to 0.125
- whitener: bfloat16 [4, 512, 512], replicated, as said below
- arc_length: int32 [4], replicated, may hold values from 1 to 512, 1536 in all
- gap_mask: int32 [4, 512], replicated, may hold values 0 or 1
- prior_diag: float32 [24576], replicated, may hold values from 0.5 to 5
Outputs:
- schur_rest: float32 [8, 3072, 24576], P(None, 'row', 'col')
- panel_factor: float32 [8, 3072, 128], P(None, 'row')
Inputs may be any that keep to these rules, and one draw needn't show every extreme that they name: `whitener`: each arc's factor is lower triangular with a positive diagonal. `arc_length`: the longest arc has exactly 512 epochs, and the lengths sum to 1536.
All inputs are finite; a program needn't handle non-finite values.
Results may differ from a plain program's by a relative error of at most 0.003.
Values may be sent and summed in bfloat16 or wider, within the bound.
A program may use at most 192 MiB of HBM per device.

v0:
```python
import jax
import jax.numpy as jnp
from jax import lax
from jax.sharding import PartitionSpec as P

PANEL = 128


def broadcast(value, axis, root):
    mine = lax.axis_index(axis) == root
    return lax.psum(jnp.where(mine, value, jnp.zeros_like(value)), axis)


def live_mask(arc_length, gap_mask):
    epoch_ids = lax.broadcasted_iota(jnp.int32, gap_mask.shape, 1)
    keep_epoch = (epoch_ids < arc_length[:, None]) & (gap_mask == 1)
    return jnp.where(keep_epoch, jnp.float32(1.0), jnp.float32(0.0))


def whiten(design_rows, whitener, weights):
    arc_count, epoch_count = weights.shape
    shaped = design_rows.reshape(arc_count, epoch_count, design_rows.shape[1])
    masked = shaped * weights[:, :, None].astype(jnp.bfloat16)
    mixed_rows = jnp.einsum("aij,ajk->aik", whitener, masked, preferred_element_type=jnp.float32)
    return (mixed_rows * weights[:, :, None]).astype(jnp.bfloat16).reshape(design_rows.shape)


def contract_rows(left_side, right_side):
    return lax.dot_general(
        left_side, right_side, (((0,), (0,)), ((), ())), preferred_element_type=jnp.float32
    )


def add_prior(matrix, row_ids, column_ids, column_prior):
    return matrix + jnp.where(
        row_ids[:, None] == column_ids[None, :], column_prior[None, :], jnp.float32(0.0)
    )


def on_device(design, whitener, arc_length, gap_mask, prior_diag):
    weights = live_mask(arc_length, gap_mask)
    row_index = lax.axis_index("row")
    col_index = lax.axis_index("col")
    row_count = lax.axis_size("row")
    col_count = lax.axis_size("col")
    col_width = design.shape[1]
    strip_width = col_width // row_count
    regrouped = lax.all_to_all(design, "row", split_axis=1, concat_axis=0, tiled=True)
    own_strip = whiten(regrouped, whitener, weights)
    column_side = lax.all_gather(own_strip, "row", axis=1, tiled=True)
    column_ids = col_index * col_width + lax.broadcasted_iota(jnp.int32, (col_width,), 0)
    column_prior = lax.dynamic_slice_in_dim(prior_diag, col_index * col_width, col_width)
    first_ids = lax.broadcasted_iota(jnp.int32, (PANEL,), 0)
    block_ids = lax.broadcasted_iota(jnp.int32, (col_count, strip_width), 0) * col_width
    block_ids = (
        block_ids
        + row_index * strip_width
        + lax.broadcasted_iota(jnp.int32, (col_count, strip_width), 1)
    ).reshape(-1)
    first_white = broadcast(own_strip[:, :PANEL], ("row", "col"), 0)
    top_rows = add_prior(
        contract_rows(first_white, column_side), first_ids, column_ids, column_prior
    )
    corner = add_prior(
        contract_rows(first_white, first_white), first_ids, first_ids, prior_diag[:PANEL]
    )
    section = lax.all_gather(own_strip, "col", axis=1, tiled=True)
    wide_tile = jnp.concatenate(
        [contract_rows(section, column_side), contract_rows(section, first_white)], axis=1
    )
    normal_tile = add_prior(wide_tile[:, :col_width], block_ids, column_ids, column_prior)
    panel_cols = add_prior(wide_tile[:, col_width:], block_ids, first_ids, prior_diag[:PANEL])
    factor = jnp.linalg.cholesky(corner)
    panel_left = lax.linalg.triangular_solve(
        factor, panel_cols, left_side=False, lower=True, transpose_a=True
    )
    panel_top = lax.linalg.triangular_solve(factor, top_rows, left_side=True, lower=True)
    schur = normal_tile - jnp.dot(
        panel_left, panel_top, precision=lax.Precision.HIGHEST, preferred_element_type=jnp.float32
    )
    return (
        schur.reshape(col_count, strip_width, col_width),
        panel_left.reshape(col_count, strip_width, PANEL),
    )


def solution(mesh):
    placed = (P("row", "col"), P(), P(), P(), P())
    return jax.shard_map(
        on_device,
        mesh=mesh,
        in_specs=placed,
        out_specs=(P(None, "row", "col"), P(None, "row", None)),
        check_vma=False,
    )
```

profile of v0, /device:TPU:0, one launch (start us, length us, event | category | flops | bytes accessed | tf_op | source)
XLA Modules:
  0.0 684.0 jit_solution(13313878694360283104)
XLA Ops:
  8.0 0.0 copy-start
  8.0 3.9 copy.11
  11.9 0.0 copy-start.4
  11.9 0.0 copy-start.5
  11.9 5.3 all-to-all-start
  17.2 0.0 all-reduce.2.cloned.1.call-start
  17.2 0.0 copy-done.4
  17.2 0.0 copy-done.5
  17.2 0.1 fusion.11
  17.3 37.1 %all-to-all-done = bf16[512,4,768]{2,0,1:T(8,128)(2,1)} async-done(((bf16[512,4,768]{2,0,1:T(8,128)(2,1)}), bf16[512,4,768]{2,0,1:T(8,128)(2,1)}, u32[]{:S(2)}, u32[]{:S(2)}) %all-to-all-start) | async-done | bytes 3145760 | tf_op jit(solution)/shard_map/all_to_all | solution.py:48
  54.4 0.0 copy-done
  54.4 5.5 multiply_convert_fusion
  59.9 1.9 slice_select_fusion
  61.7 0.0 all-reduce.2.cloned.1.call-update
  61.8 0.0 all-gather.5.cloned.1.call-start
  61.8 0.5 all-gather.5.cloned.1.call-update
  62.3 0.2 all-gather.3.cloned.1.call-start
  62.6 0.4 all-gather.3.cloned.1.call-update
  62.9 0.7 slice.22
  63.6 0.7 dynamic_slice.3
  64.3 0.1 iota_add_fusion
  64.4 398.9 %all-reduce.2.cloned.1.call-done = bf16[2048,128]{1,0:T(8,128)(2,1)} async-done(((bf16[2048,128]{1,0:T(8,128)(2,1)}), bf16[2048,128]{1,0:T(8,128)(2,1)}) %all-reduce.2.cloned.1.call-update) | async-done | bytes 524304 | tf_op jit(solution)/shard_map/psum | solution.py:11
  463.3 1.5 fusion.13
  464.8 0.1 copy.8
  464.9 0.1 fusion.8
  465.0 11.7 %cholesky.16 = f32[128,128]{1,0:T(8,128)S(1)} custom-call(f32[128,128]{1,0:T(8,128)S(1)} %fusion.8), custom_call_target="Cholesky" | custom-call | tf_op jit(solution)/shard_map/jit(cholesky)/cholesky | solution.py:73
  476.8 0.6 compare_reduce_fusion
  477.4 0.7 fusion.2
  478.1 9.8 %custom-call.8 = f32[1,128,128]{1,2,0:T(8,128)S(1)} custom-call(f32[1,128,128]{2,1,0:T(8,128)S(1)} %fusion.2), custom_call_target="InvertDiagBlocksLowerTriangular" | custom-call | tf_op jit(solution)/shard_map/triangular_solve | solution.py:74
  487.9 0.0 all-gather.5.cloned.1.call-done
  487.9 6.6 convolution_add_fusion.1
  494.5 0.0 copy-start.3
  494.5 2.6 fusion.3
  497.1 0.0 all-gather.3.cloned.1.call-done
  497.2 0.0 copy-done.3
  497.2 12.1 %convolution_add_fusion = f32[6144,128]{1,0:T(8,128)S(1)} fusion(bf16[2048,6144]{1,0:T(8,128)(2,1)} %all-gather.3.cloned.1.call-done, bf16[2048,128]{1,0:T(8,128)(2,1)S(1)} %copy-done.3, f32[128]{0:T(128)S(1)} %slice.22, s32[6144]{0:T(1024)S(1)} %add.71), kind=kOutput, calls=%fused_computation.1 | convolution fusion | flops 3223584768 | bytes 28860928 | tf_op jit(solution)/shard_map/dot_general | solution.py:29
  509.2 0.0 copy-start.2
  509.2 2.6 fusion.5
  511.8 0.0 copy-start.1
  511.9 1.7 copy-done.1
  513.5 0.0 copy-done.2
  513.5 64.4 %fusion.14 = f32[6144,3072]{1,0:T(8,128)} fusion(f32[6144,128]{1,0:T(8,128)S(1)} %fusion.5, f32[128,3072]{1,0:T(8,128)S(1)} %copy-done.2), kind=kOutput, calls=%fused_computation.33 | convolution fusion | flops 28991029248 | bytes 80216064 | tf_op jit(solution)/shard_map/dot_general | solution.py:78
  578.0 98.2 %add_subtract_fusion = f32[6144,3072]{1,0:T(8,128)} fusion(f32[6144,3072]{1,0:T(8,128)} %fusion.14, bf16[2048,6144]{1,0:T(8,128)(2,1)} %all-gather.3.cloned.1.call-done, bf16[2048,3072]{1,0:T(8,128)(2,1)} %all-gather.5.cloned.1.call-done, f32[3072]{0:T(1024)S(1)} %dynamic_slice.3, s32[3072]{0:T(1024)S(1)} %iota_add_fusion.1, s32[6144]{0:T(1024)S(1)} %add.71), kind=kOutput, calls=%fused_computation | convolution fusion | flops 77384908800 | bytes 188792832 | tf_op jit(solution)/shard_map/dot_general | solution.py:29
  (4 shorter events, 0.1 us)
Async XLA Ops:
  8.0 46.4 %copy-start = (bf16[4,512,512]{2,1,0:T(8,128)(2,1)S(1)}, bf16[4,512,512]{2,1,0:T(8,128)(2,1)}, u32[]{:S(2)}) copy-start(bf16[4,512,512]{2,1,0:T(8,128)(2,1)} %param.6) | copy-start | bytes 6291460
  11.9 5.3 copy-start.4
  11.9 5.3 copy-start.5
  11.9 42.5 %all-to-all-start = ((bf16[512,4,768]{2,0,1:T(8,128)(2,1)}), bf16[512,4,768]{2,0,1:T(8,128)(2,1)}, u32[]{:S(2)}, u32[]{:S(2)}) async-start(bf16[512,4,768]{2,0,1:T(8,128)(2,1)} %bitcast.44), calls=%async_computation | async-start | bytes 6291456 | tf_op jit(solution)/shard_map/all_to_all | solution.py:48
  17.2 446.1 %all-reduce.2.cloned.1.call-start = ((), (), s32[]{:S(2)}) async-start(), calls=%async_computation.3 | async-start | bytes 1048576 | tf_op jit(solution)/shard_map/psum | solution.py:11
  61.8 426.1 %all-gather.5.cloned.1.call-start = ((), (), s32[]{:S(2)}) async-start(), calls=%async_computation.2 | async-start | bytes 15728640 | tf_op jit(solution)/shard_map/all_gather | solution.py:50
  62.3 434.8 %all-gather.3.cloned.1.call-start = ((), (), s32[]{:S(2)}) async-start(), calls=%async_computation.1 | async-start | bytes 28311552 | tf_op jit(solution)/shard_map/all_gather | solution.py:67
  494.5 2.6 copy-start.3
  509.2 4.3 copy-start.2
  511.8 1.7 copy-start.1
Sparse Core Ops, SparseCore 0:
  61.9 401.3 all-reduce.1
Sparse Core Ops, SparseCore 1:
  64.7 123.1 all-gather.4
  189.9 220.1 all-gather.2
where the time goes:
time: 692 us; the launch traced here: 684 us
  waiting for transfers between devices  437 us (63%)
  matrix products  194 us (28%)
  other arithmetic  25 us (4%)
  between operations  16 us (2%)
  local copies, waits for them, and re-layouts  7.08 us (1%)
    psum x1, waiting for transfers between devices, broadcast(): return lax.psum(jnp.where(mine, value, jnp.zeros_like(value)), axis)  399 us
    dot_general x4, matrix products, contract_rows(): lax.dot_general(left_side, right_side, (((0,), (0,)), ((), ())), preferre...  118 us
    dot_general x1, matrix products, on_device(): jnp.dot(panel_left, panel_top, precision=lax.Precision.HIGHEST, preferred...  64.4 us
    all_to_all x1, waiting for transfers between devices, on_device(): lax.all_to_all(design, 'row', split_axis=1, concat_axis=0, tiled=True)  37.1 us
  transfers between devices with their start and end apart: 4, of which 2 were waited for; matrix products, arithmetic and copies ran while one was open for 5% of the time, Pallas kernels for 0%

commit v1 on v0

--- a/solution.py
+++ b/solution.py
@@ -1,9 +1,270 @@
+import functools
+
 import jax
 import jax.numpy as jnp
+import numpy as np
 from jax import lax
+from jax.experimental import pallas as pl
+from jax.experimental.pallas import tpu as pltpu
 from jax.sharding import PartitionSpec as P
 
 PANEL = 128
+LANES = 128
+F32 = jnp.float32
+BF16 = jnp.bfloat16
+EXACT = lax.Precision.HIGHEST
+
+
+def params(**more):
+    return pltpu.CompilerParams(vmem_limit_bytes=48 * 2**20, **more)
+
+
+def cost(flops, nbytes):
+    return pl.CostEstimate(flops=int(flops), bytes_accessed=int(nbytes), transcendentals=0)
+
+
+def iota(shape, dim):
+    return lax.broadcasted_iota(jnp.int32, shape, dim)
+
+
+def split_two(value):
+    high = value.astype(BF16)
+    return high, (value - high.astype(F32)).astype(BF16)
+
+
+def live_mask(arc_length, gap_mask):
+    return (iota(gap_mask.shape, 1) < arc_length[:, None]) & (gap_mask == 1)
+
+
+def compact_whitener(whitener, live, kept):
+    arcs, epochs = live.shape
+    flat = live.reshape(-1)
+    place = (jnp.cumsum(flat.astype(jnp.int32)) - 1).reshape(arcs, 1, epochs)
+    pick = (iota((arcs, kept, epochs), 1) == place) & live[:, None, :]
+    rows = jnp.einsum("ake,aef->akf", pick.astype(BF16), whitener, preferred_element_type=F32)
+    return jnp.where(live[:, None, :], rows, 0.0).astype(BF16)
+
+
+def whiten_kernel(order_ref, mixer_ref, *refs):
+    blocks, out_ref = refs[:-1], refs[-1]
+    total = jnp.dot(mixer_ref[order_ref[0]], blocks[0][...], preferred_element_type=F32)
+    for s in range(1, len(blocks)):
+        total += jnp.dot(mixer_ref[order_ref[s]], blocks[s][...], preferred_element_type=F32)
+    out_ref[...] = total.astype(BF16)
+
+
+def whiten(order, mixer, blocks):
+    arcs, kept, epochs = mixer.shape
+    width = blocks[0].shape[1]
+    part = kept // 2
+    return pl.pallas_call(
+        whiten_kernel,
+        grid_spec=pltpu.PrefetchScalarGridSpec(
+            num_scalar_prefetch=1,
+            grid=(2,),
+            in_specs=[pl.BlockSpec((arcs, part, epochs), lambda i, o: (0, i, 0))]
+            + [pl.BlockSpec(b.shape, lambda i, o: (0, 0)) for b in blocks],
+            out_specs=pl.BlockSpec((part, width), lambda i, o: (i, 0)),
+        ),
+        out_shape=jax.ShapeDtypeStruct((kept, width), BF16),
+        compiler_params=params(),
+        cost_estimate=cost(2 * kept * arcs * epochs * width, 2 * arcs * epochs * (kept + width)),
+        name="whiten",
+    )(order, mixer, *blocks)
+
+
+def factor_kernel(first_ref, prior_ref, inv_ref, inv_t_ref):
+    first = first_ref[...]
+    n = first.shape[1]
+    same = iota((n, n), 0) == iota((n, n), 1)
+    corner = jnp.dot(first.T, first, preferred_element_type=F32)
+    corner = corner + jnp.where(same, prior_ref[...], 0.0)
+    rows, lanes = iota((n, n), 0), iota((n, n), 1)
+    row_ids = iota((n, 1), 0)
+
+    def step(k, held):
+        a, r = held
+        at_row = rows == k
+        a_row = jnp.sum(jnp.where(at_row, a, 0.0), axis=0, keepdims=True)
+        r_row = jnp.sum(jnp.where(at_row, r, 0.0), axis=0, keepdims=True)
+        column = jnp.sum(jnp.where(lanes == k, a, 0.0), axis=1, keepdims=True)
+        pivot = jnp.sum(jnp.where(lanes[:1] == k, a_row, 0.0), axis=1, keepdims=True)
+        share = jnp.where(row_ids > k, column / pivot, 0.0)
+        return a - share * a_row, r - share * r_row
+
+    a, r = lax.fori_loop(0, n, step, (corner, jnp.where(same, 1.0, 0.0).astype(F32)))
+    diagonal = jnp.sum(jnp.where(same, a, 0.0), axis=1, keepdims=True)
+    inverse = r / jnp.sqrt(diagonal)
+    inv_ref[...] = inverse
+    inv_t_ref[...] = inverse.T
+
+
+def factor_inverse(first, prior):
+    n = first.shape[1]
+    square = jax.ShapeDtypeStruct((n, n), F32)
+    return pl.pallas_call(
+        factor_kernel,
+        out_shape=(square, square),
+        compiler_params=params(),
+        cost_estimate=cost(2e10, 2 * first.size),
+        name="factor_inverse",
+    )(first, prior)
+
+
+def right_kernel(kept, count, where_ref, first_ref, prior_ref, inv_ref, *refs):
+    parts, out_ref = refs[:count], refs[-1]
+    strip = jnp.concatenate([p[...] for p in parts], axis=0) if count > 1 else parts[0][...]
+    rows, width = strip.shape
+    n = first_ref.shape[1]
+    top = jnp.dot(first_ref[...].T, strip, preferred_element_type=F32)
+    same = (iota((n, width), 0) == iota((n, width), 1)) & (where_ref[0] == 0)
+    top = top + jnp.where(same, prior_ref[...], 0.0)
+    solved = jnp.dot(inv_ref[...], top, precision=EXACT, preferred_element_type=F32)
+    high, low = split_two(solved)
+    out_ref[0, :rows] = strip
+    if kept > rows:
+        out_ref[0, rows:kept] = jnp.zeros((kept - rows, width), BF16)
+    out_ref[0, kept : kept + n] = high
+    out_ref[0, kept + n : kept + 2 * n] = low
+    out_ref[0, kept + 2 * n :] = high
+
+
+def right_side(kept, slot, slots, column, first, prior, inverse, parts, held):
+    width = parts[0].shape[1]
+    n = first.shape[1]
+    depth = kept + 3 * n
+    whole = lambda a: pl.BlockSpec(a.shape, lambda i, w: (0,) * a.ndim)
+    operands = [first, prior, inverse] + list(parts)
+    specs = [whole(a) for a in operands]
+    aliases = {}
+    if held is not None:
+        aliases = {1 + len(operands): 0}
+        operands.append(held)
+        specs.append(pl.BlockSpec(memory_space=pl.ANY))
+    return pl.pallas_call(
+        functools.partial(right_kernel, kept, len(parts)),
+        grid_spec=pltpu.PrefetchScalarGridSpec(
+            num_scalar_prefetch=1,
+            grid=(1,),
+            in_specs=specs,
+            out_specs=pl.BlockSpec((1, depth, width), lambda i, w: (slot, 0, 0)),
+        ),
+        out_shape=jax.ShapeDtypeStruct((slots, depth, width), BF16),
+        input_output_aliases=aliases,
+        compiler_params=params(),
+        cost_estimate=cost(2 * n * width * (kept + 6 * n), 4 * depth * width),
+        name="right_side",
+    )(column, *operands)
+
+
+def tile_kernel(kept, choices, at_ref, order_ref, *refs):
+    candidates = [refs[2 * q : 2 * q + 2] for q in range(choices)]
+    refs = refs[2 * choices :]
+    right_ref, first_ref, prior_ref, first_prior_ref, inv_t_ref = refs[:5]
+    schur_ref, panel_ref, landed, left, sems = refs[-5:]
+    s, i = pl.program_id(0), pl.program_id(1)
+    rows = candidates[0][0].shape[0]
+    width = left.shape[1]
+    n = first_ref.shape[1]
+    block = at_ref[0] * 2 + (i ^ at_ref[4])
+    row_index, col_index, choice = at_ref[1], at_ref[2], at_ref[3]
+
+    @pl.when((s == 0) & (i == 0))
+    def _():
+        if kept > rows:
+            for g in range(2):
+                landed[g, rows:kept] = jnp.zeros((kept - rows, width), BF16)
+        for q in range(choices):
+
+            @pl.when(choice == q)
+            def _():
+                for g in range(2):
+                    pltpu.make_async_copy(
+                        candidates[q][g], landed.at[g, pl.ds(0, rows)], sems.at[g]
+                    ).start()
+
+    @pl.when(s == 0)
+    def _():
+        pltpu.make_async_copy(
+            candidates[0][0], landed.at[i, pl.ds(0, rows)], sems.at[i]
+        ).wait()
+        turned = landed[i].T
+        left[i, :, :kept] = turned
+        near = jnp.dot(turned, first_ref[...], preferred_element_type=F32)
+        same = (iota((width, n), 0) == iota((width, n), 1)) & (block + row_index == 0)
+        near = near + jnp.where(same, first_prior_ref[...], 0.0)
+        solved = jnp.dot(near, inv_t_ref[...], precision=EXACT, preferred_element_type=F32)
+        panel_ref[0] = solved
+        high, low = split_two(-solved)
+        left[i, :, kept : kept + n] = high
+        left[i, :, kept + n : kept + 2 * n] = high
+        left[i, :, kept + 2 * n :] = low
+
+    schur_ref[0] = jnp.dot(left[i], right_ref[0], preferred_element_type=F32)
+
+    @pl.when((block == col_index) & (s == 0))
+    def _():
+        same = iota((width, width), 0) == iota((width, width), 1)
+        schur_ref[0] = schur_ref[0] + jnp.where(same, prior_ref[...], 0.0)
+
+
+def tiles(kept, at, order, pairs, right, first, prior, first_prior, inv_t, blocks, held):
+    slots, depth, width = right.shape
+    rows = pairs[0][0].shape[0]
+    n = first.shape[1]
+    whole = lambda a: pl.BlockSpec(a.shape, lambda s, i, at, order: (0,) * a.ndim)
+    anywhere = pl.BlockSpec(memory_space=pl.ANY)
+    operands = [half for pair in pairs for half in pair]
+    specs = [anywhere] * len(operands)
+    operands += [right, first, prior, first_prior, inv_t]
+    specs += [pl.BlockSpec((1, depth, width), lambda s, i, at, order: (s, 0, 0))]
+    specs += [whole(a) for a in operands[-4:]]
+    aliases = {}
+    if held is not None:
+        aliases = {2 + len(operands): 0, 3 + len(operands): 1}
+        operands += list(held)
+        specs += [anywhere] * 2
+    return pl.pallas_call(
+        functools.partial(tile_kernel, kept, len(pairs)),
+        grid_spec=pltpu.PrefetchScalarGridSpec(
+            num_scalar_prefetch=2,
+            grid=(slots, 2),
+            in_specs=specs,
+            out_specs=[
+                pl.BlockSpec(
+                    (1, width, width),
+                    lambda s, i, at, order: (at[0] * 2 + (i ^ at[4]), 0, order[s]),
+                ),
+                pl.BlockSpec(
+                    (1, width, n),
+                    lambda s, i, at, order: (at[0] * 2 + (jnp.where(s == 0, i, 1) ^ at[4]), 0, 0),
+                ),
+            ],
+            scratch_shapes=[
+                pltpu.VMEM((2, kept, width), BF16),
+                pltpu.VMEM((2, width, depth), BF16),
+                pltpu.SemaphoreType.DMA((2,)),
+            ],
+        ),
+        out_shape=(
+            jax.ShapeDtypeStruct((blocks, width, slots * width), F32),
+            jax.ShapeDtypeStruct((blocks, width, n), F32),
+        ),
+        input_output_aliases=aliases,
+        compiler_params=params(),
+        cost_estimate=cost(
+            4 * width * width * slots * depth, 8 * width * width * slots + 2 * right.size
+        ),
+        name="tiles",
+    )(at, order, *operands)
+
+
+def line_schedule(chips):
+    table = []
+    for z in range(chips):
+        others = [(abs(q - z), int(q > z), q) for q in range(chips) if q != z]
+        table.append([(q, side, d) for d, side, q in sorted(others)])
+    return table
 
 
 def broadcast(value, axis, root):
@@ -11,13 +272,7 @@
     return lax.psum(jnp.where(mine, value, jnp.zeros_like(value)), axis)
 
 
-def live_mask(arc_length, gap_mask):
-    epoch_ids = lax.broadcasted_iota(jnp.int32, gap_mask.shape, 1)
-    keep_epoch = (epoch_ids < arc_length[:, None]) & (gap_mask == 1)
-    return jnp.where(keep_epoch, jnp.float32(1.0), jnp.float32(0.0))
-
-
-def whiten(design_rows, whitener, weights):
+def whiten_rows(design_rows, whitener, weights):
     arc_count, epoch_count = weights.shape
     shaped = design_rows.reshape(arc_count, epoch_count, design_rows.shape[1])
     masked = shaped * weights[:, :, None].astype(jnp.bfloat16)
@@ -37,8 +292,8 @@
     )
 
 
-def on_device(design, whitener, arc_length, gap_mask, prior_diag):
-    weights = live_mask(arc_length, gap_mask)
+def by_blocks(design, whitener, arc_length, gap_mask, prior_diag):
+    weights = jnp.where(live_mask(arc_length, gap_mask), jnp.float32(1.0), jnp.float32(0.0))
     row_index = lax.axis_index("row")
     col_index = lax.axis_index("col")
     row_count = lax.axis_size("row")
@@ -46,7 +301,7 @@
     col_width = design.shape[1]
     strip_width = col_width // row_count
     regrouped = lax.all_to_all(design, "row", split_axis=1, concat_axis=0, tiled=True)
-    own_strip = whiten(regrouped, whitener, weights)
+    own_strip = whiten_rows(regrouped, whitener, weights)
     column_side = lax.all_gather(own_strip, "row", axis=1, tiled=True)
     column_ids = col_index * col_width + lax.broadcasted_iota(jnp.int32, (col_width,), 0)
     column_prior = lax.dynamic_slice_in_dim(prior_diag, col_index * col_width, col_width)
@@ -84,10 +339,117 @@
     )
 
 
+def on_device(design, whitener, arc_length, gap_mask, prior_diag):
+    live = live_mask(arc_length, gap_mask)
+    row_index = lax.axis_index("row")
+    col_index = lax.axis_index("col")
+    rows = lax.axis_size("row")
+    cols = lax.axis_size("col")
+    chips = cols // 2
+    arcs, epochs = live.shape
+    col_width = design.shape[1]
+    width = col_width // rows
+    chip = col_index // 2
+    order = row_index ^ jnp.arange(rows, dtype=jnp.int32)
+
+    def swap_row(value, mask):
+        return lax.ppermute(value, "row", [(r, r ^ mask) for r in range(rows)])
+
+    def swap_core(value):
+        return lax.ppermute(value, "col", [(c, c ^ 1) for c in range(cols)])
+
+    def shift(value, step):
+        pairs = [(c, c + 2 * step) for c in range(cols) if 0 <= c + 2 * step < cols]
+        return lax.ppermute(value, "col", pairs)
+
+    def strip_of(index):
+        return lax.dynamic_slice_in_dim(design, index * width, width, axis=1)
+
+    raw = [strip_of(row_index)]
+    for s in range(1, rows):
+        raw.append(swap_row(strip_of(row_index ^ s), s))
+
+    column_prior = lax.dynamic_slice_in_dim(
+        prior_diag, col_index * col_width + row_index * width, width
+    ).reshape(1, width)
+    first_prior = prior_diag[:PANEL]
+    table = line_schedule(chips)
+
+    def run(sent, raw):
+        kept = -(-sent // LANES) * LANES
+        own = whiten(order, compact_whitener(whitener, live, sent), raw)
+
+        mine = (row_index == 0) & (col_index == 0)
+        first = jnp.where(mine, own[:, :PANEL], jnp.zeros((sent, PANEL), BF16))
+        first = lax.psum(first, ("row", "col"))
+
+        moving = {0: own, 1: own}
+        arrived = {}
+        for t in range(1, chips):
+            moving = {0: shift(moving[0], 1), 1: shift(moving[1], -1)}
+            arrived[0, t], arrived[1, t] = moving[0], moving[1]
+
+        core = col_index % 2
+
+        near = [own] + [swap_row(own, 1 << b) for b in range((rows - 1).bit_length())]
+        half = sent // 32 * 16
+        strips = {0: [own], 1: [near[1]], 2: [near[2]]}
+        strips[3] = [swap_row(near[2][:half], 1), swap_row(near[1][half:], 2)]
+
+        inverse, inv_t = factor_inverse(first, first_prior.reshape(1, PANEL))
+        wide = jnp.pad(first, ((0, kept - sent), (0, 0)))
+        top_prior = first_prior.reshape(PANEL, 1)
+        right = None
+        for s in range(rows):
+            spot = (col_index + (row_index ^ s)).reshape(1)
+            right = right_side(
+                kept, s, rows, spot, first, top_prior, inverse, strips[s], right
+            )
+
+        held = None
+        sibling = {0: swap_core(own)}
+        for key, value in arrived.items():
+            sibling[key] = swap_core(value)
+        for t in range(chips):
+            if t == 0:
+                keys, target, choice = [0], chip, jnp.int32(0)
+                source = {0: own}
+            else:
+                wanted = [table[z][t - 1] for z in range(chips)]
+                keys = sorted({(side, d) for _, side, d in wanted})
+                target = jnp.asarray(np.array([q for q, _, _ in wanted], np.int32))[chip]
+                choice = jnp.asarray(
+                    np.array([keys.index((side, d)) for _, side, d in wanted], np.int32)
+                )[chip]
+                source = arrived
+            pairs = [(source[k], sibling[k]) for k in keys]
+            at = jnp.stack([target, row_index, col_index, choice, core]).astype(jnp.int32)
+            held = tiles(
+                kept, at, order, pairs, right, wide, column_prior,
+                first_prior.reshape(1, PANEL), inv_t, cols, held,
+            )
+        return held
+
+    most = 3 * epochs
+    sizes = [most * 19 // 24, most]
+    count = jnp.sum(live.astype(jnp.int32))
+    return lax.switch(
+        jnp.where(count <= sizes[0], 0, 1),
+        [functools.partial(run, size) for size in sizes],
+        raw,
+    )
+
+
 def solution(mesh):
+    def run(design, whitener, arc_length, gap_mask, prior_diag):
+        rows = lax.axis_size("row")
+        fits = rows == 4 and whitener.shape[0] == rows and design.shape[1] % (rows * LANES) == 0
+        form = on_device if fits else by_blocks
+        return form(design, whitener, arc_length, gap_mask, prior_diag)
+
     placed = (P("row", "col"), P(), P(), P(), P())
     return jax.shard_map(
-        on_device,
+        run,
         mesh=mesh,
         in_specs=placed,
         out_specs=(P(None, "row", "col"), P(None, "row", None)),

time: 692 us -> 420 us (0.61)
  waiting for transfers between devices: 437 us -> 179 us
  matrix products: 194 us -> 6.04 us
  Pallas kernels: 0 us -> 148 us
  starting transfers between devices: 5.55 us -> 31.6 us
  other arithmetic: 25 us -> 2.75 us
  local copies, waits for them, and re-layouts: 7.08 us -> 21.5 us
  loops' own time: 0 us -> 8.99 us
    psum x1, waiting for transfers between devices: 399 us -> 91.7 us  [run(): first = lax.psum(first, ('row', 'col'))]
    dot_general x6 -> x1, matrix products: 188 us -> 6.04 us  [compact_whitener(): jnp.einsum('ake,aef->akf', pick.astype(BF16), whitener, preferred_element...]
    pallas_call x0 -> x10, Pallas kernels: none -> 148 us  [the longest x4 110 us: tiles(): pl.pallas_call(functools.partial(tile_kernel, kept, len(pairs)), grid_spe...]
    ppermute x0 -> x20, waiting for transfers between devices: none -> 87.1 us  [the longest x6 44.7 us: shift(): return lax.ppermute(value, 'col', pairs)]
    all_to_all x1 -> x0, waiting for transfers between devices: 37.1 us -> none  [on_device(): lax.all_to_all(design, 'row', split_axis=1, concat_axis=0, tiled=True)]
    ppermute x0 -> x20, starting transfers between devices: none -> 31.6 us  [the longest x6 22 us: shift(): return lax.ppermute(value, 'col', pairs)]
    another operation x5 -> x2, other arithmetic: 22.9 us -> 0.32 us  [the longest x3 12.4 us: on_device(): factor = jnp.linalg.cholesky(corner)]
    another operation x0 -> x1, loops' own time: none -> 8.99 us  [on_device(): lax.switch(jnp.where(count <= sizes[0], 0, 1), [functools.partial(run, si...]
  transfers between devices with their start and end apart: 4 -> 21, of which waited for: 2 -> 7; matrix products, arithmetic and copies ran while one was open for 5% -> 3% of each run, Pallas kernels for 0% -> 27%
where the time goes in v1:
time: 420 us; the launch traced here: 413 us
  waiting for transfers between devices  179 us (43%)
  Pallas kernels  148 us (35%)
  starting transfers between devices  31.6 us (8%)
  local copies, waits for them, and re-layouts  21.5 us (5%)
  between operations  15 us (4%)
  loops' own time  8.99 us (2%)
  matrix products  6.04 us (1%)
    pallas_call x4, Pallas kernels, tiles(): pl.pallas_call(functools.partial(tile_kernel, kept, len(pairs)), grid_spe...  110 us
    psum x1, waiting for transfers between devices, run(): first = lax.psum(first, ('row', 'col'))  91.7 us
    ppermute x6, waiting for transfers between devices, shift(): return lax.ppermute(value, 'col', pairs)  44.7 us
    ppermute x7, waiting for transfers between devices, swap_row(): return lax.ppermute(value, 'row', [(r, r ^ mask) for r in range(rows)])  42.4 us
    ppermute x6, starting transfers between devices, shift(): return lax.ppermute(value, 'col', pairs)  22 us
    pallas_call x1, Pallas kernels, factor_inverse(): pl.pallas_call(factor_kernel, out_shape=(square, square), compiler_params...  16.8 us
    pallas_call x4, Pallas kernels, right_side(): pl.pallas_call(functools.partial(right_kernel, kept, len(parts)), grid_sp...  12.7 us
    another operation x1, loops' own time, on_device(): lax.switch(jnp.where(count <= sizes[0], 0, 1), [functools.partial(run, si...  8.99 us
  transfers between devices with their start and end apart: 21, of which 7 were waited for; matrix products, arithmetic and copies ran while one was open for 3% of the time, Pallas kernels for 27%

profile of v1, /device:TPU:0, one launch (start us, length us, event | category | flops | bytes accessed | tf_op | source)
XLA Modules:
  0.0 412.8 jit_solution(3546461003221845081)
XLA Ops:
  7.2 1.8 constant_dynamic-slice_fusion.4
  9.0 3.0 collective-permute-start.34
  12.0 1.5 collective-permute-start.35
  13.5 0.7 convert_reduce_fusion
  14.9 15.6 %collective-permute-done.34 = bf16[512,768]{1,0:T(8,128)(2,1)} collective-permute-done((bf16[512,768]{1,0:T(8,128)(2,1)S(1)}, bf16[512,768]{1,0:T(8,128)(2,1)}, u32[]{:S(2)}, u32[]{:S(2)}) %collective-permute-start.34) | collective-permute-done | bytes 786464 | tf_op jit(solution)/shard_map/ppermute | solution.py:356
  30.5 17.5 %collective-permute-done.35 = bf16[512,768]{1,0:T(8,128)(2,1)} collective-permute-done((bf16[512,768]{1,0:T(8,128)(2,1)S(1)}, bf16[512,768]{1,0:T(8,128)(2,1)}, u32[]{:S(2)}, u32[]{:S(2)}) %collective-permute-start.35) | collective-permute-done | bytes 786464 | tf_op jit(solution)/shard_map/ppermute | solution.py:356
  48.0 357.7 %conditional.1 = ((f32[8,768,3072]{2,1,0:T(8,128)}, f32[8,768,128]{2,1,0:T(8,128)})) conditional(s32[]{:T(128)} %clamp.3, (s32[]{:T(128)}, (), s32[]{:T(128)}, s32[]{:T(128)}, (), /*index=5*/pred[4,512]{1,0:T(4,128)(4,1)S(1)}, bf16[4,512,512]{2,1,0:T(8,128)(2,1)}, s32[]{:T(128)}, bf16[512,3072]{1,0:T(8,128)(2,1)}, bf16[512,768]{1,0:T(8,128)(2,1)}, ...), branch_computations={%region_1.5_spmd, %region_5.9_spmd} | conditional | flops 102355820544 | bytes 394253152 | solution.py:436
  48.0 0.3 reduce-window.12
  48.3 0.1 slice.38
  48.4 0.1 slice_reduce_fusion
  48.5 0.1 reshape.108
  48.6 0.1 broadcast_bitcast_fusion
  48.7 6.0 %select_convert_fusion.mixer_ref = bf16[4,1216,512]{2,1,0:T(8,128)(2,1)} fusion(bf16[4,512,512]{2,1,0:T(8,128)(2,1)} %get-tuple-element.178, s32[4,512]{1,0:T(4,128)S(1)} %fusion.7, pred[4,512]{1,0:T(4,128)(4,1)S(1)} %get-tuple-element.78), kind=kOutput, calls=%fused_computation | convolution fusion | flops 2560098304 | bytes 7088128 | tf_op jit(solution)/shard_map/cond/branch_0_fun/ake,aef->akf/dot_general | solution.py:44
  54.7 1.6 constant_dynamic-slice_fusion.refs_0_
  56.4 8.1 %whiten.2.refs_0_ = bf16[1216,768]{1,0:T(8,128)(2,1)} custom-call(s32[4]{0:T(128)S(1)} %broadcast_xor_fusion.order_ref, bf16[4,1216,512]{2,1,0:T(8,128)(2,1)} %select_convert_fusion.mixer_ref, bf16[512,768]{1,0:T(8,128)(2,1)S(1)} %constant_dynamic-slice_fusion.refs_0_, bf16[512,768]{1,0:T(8,128)(2,1)} %get-tuple-element.81.refs_1_, ...), custom_call_target="tpu_custom_call" | custom-call | flops 3825205248 | bytes 8126464 | tf_op jit(solution)/shard_map/cond/branch_0_fun/whiten/pallas_call | solution.py:60
  64.5 1.4 collective-permute-start.5
  66.0 5.8 %collective-permute-start = (bf16[1216,768]{1,0:T(8,128)(2,1)}, bf16[1216,768]{1,0:T(8,128)(2,1)}, u32[]{:S(2)}, u32[]{:S(2)}) collective-permute-start(bf16[1216,768]{1,0:T(8,128)(2,1)} %whiten.2.refs_0_), channel_id=1, source_target_pairs={{0,2},{1,3},{2,4},{3,5},{4,6},{5,7},{8,10},{9,11},{10,12},{11,13},... | collective-permute-start | bytes 5603336 | tf_op jit(solution)/shard_map/cond/branch_0_fun/ppermute | solution.py:363
  71.8 1.5 collective-permute-start.10
  73.3 0.5 collective-permute-start.12
  73.8 34.3 %collective-permute-done.5.refs_2_ = bf16[1216,768]{1,0:T(8,128)(2,1)S(1)} collective-permute-done((bf16[1216,768]{1,0:T(8,128)(2,1)}, bf16[1216,768]{1,0:T(8,128)(2,1)S(1)}, u32[]{:S(2)}, u32[]{:S(2)}) %collective-permute-start.5) | collective-permute-done | bytes 1867808 | tf_op jit(solution)/shard_map/cond/branch_0_fun/ppermute | solution.py:363
  108.1 1.3 collective-permute-start.6
  109.4 5.8 %collective-permute-start.1 = (bf16[1216,768]{1,0:T(8,128)(2,1)}, bf16[1216,768]{1,0:T(8,128)(2,1)}, u32[]{:S(2)}, u32[]{:S(2)}) collective-permute-start(bf16[1216,768]{1,0:T(8,128)(2,1)} %collective-permute-done.refs_0_), channel_id=1, source_target_pairs={{0,2},{1,3},{2,4},{3,5},{4,6},{5,7},{8,10},{9,11},{10,12},{11,13},... | collective-permute-start | bytes 5603336 | tf_op jit(solution)/shard_map/cond/branch_0_fun/ppermute | solution.py:363
  115.3 1.0 slice.41
  116.3 1.2 copy-done.8
  117.5 1.4 collective-permute-start.11
  119.0 1.0 slice.42
  119.9 1.2 copy-done.10
  121.2 0.5 collective-permute-start.13
  121.7 1.7 slice_select_fusion
  123.5 0.7 slice_bitcast_fusion
  124.1 0.1 copy.66.prior_ref
  124.3 0.8 dynamic_slice.58
  125.1 0.7 dynamic_slice.38
  125.7 0.6 dynamic_slice.39
  126.3 0.6 dynamic_slice.36
  126.9 0.6 dynamic_slice.37
  127.5 0.6 dynamic_slice.34
  128.1 0.6 dynamic_slice.35
  128.7 0.1 stack.40.at_ref
  128.8 1.3 stack.38.at_ref
  130.1 1.3 stack.37.at_ref
  131.4 1.3 stack.36.at_ref
  132.7 5.4 %collective-permute-done.11.refs_0_ = bf16[608,768]{1,0:T(8,128)(2,1)S(1)} collective-permute-done((bf16[608,768]{1,0:T(8,128)(2,1)}, bf16[608,768]{1,0:T(8,128)(2,1)S(1)}, u32[]{:S(2)}, u32[]{:S(2)}) %collective-permute-start.11) | collective-permute-done | bytes 933920 | tf_op jit(solution)/shard_map/cond/branch_0_fun/ppermute | solution.py:356
  138.1 3.9 collective-permute-done.13.refs_1_
  142.0 10.3 %collective-permute-done.6.refs_4_ = bf16[1216,768]{1,0:T(8,128)(2,1)} collective-permute-done((bf16[1216,768]{1,0:T(8,128)(2,1)S(1)}, bf16[1216,768]{1,0:T(8,128)(2,1)}, u32[]{:S(2)}, u32[]{:S(2)}) %collective-permute-start.6) | collective-permute-done | bytes 1867808 | tf_op jit(solution)/shard_map/cond/branch_0_fun/ppermute | solution.py:363
  152.3 1.3 collective-permute-start.8
  153.7 6.4 %collective-permute-start.3 = (bf16[1216,768]{1,0:T(8,128)(2,1)}, bf16[1216,768]{1,0:T(8,128)(2,1)}, u32[]{:S(2)}, u32[]{:S(2)}) collective-permute-start(bf16[1216,768]{1,0:T(8,128)(2,1)} %collective-permute-done.1.refs_0_), channel_id=1, source_target_pairs={{0,2},{1,3},{2,4},{3,5},{4,6},{5,7},{8,10},{9,11},{10,12},{11,13},... | collective-permute-start | bytes 5603336 | tf_op jit(solution)/shard_map/cond/branch_0_fun/ppermute | solution.py:363
  160.0 91.7 %all-reduce.4.cloned.1.call-done.first_ref = bf16[1216,128]{1,0:T(8,128)(2,1)} async-done(((bf16[1216,128]{1,0:T(8,128)(2,1)}), bf16[1216,128]{1,0:T(8,128)(2,1)}) %all-reduce.4.cloned.1.call-update) | async-done | bytes 311312 | tf_op jit(solution)/shard_map/cond/branch_0_fun/psum | solution.py:384
  251.7 1.0 copy-done.2
  252.7 16.8 %factor_inverse.2 = (f32[128,128]{1,0:T(8,128)S(1)}, f32[128,128]{1,0:T(8,128)S(1)}) custom-call(bf16[1216,128]{1,0:T(8,128)(2,1)S(1)} %copy-done.2, f32[1,128]{1,0:T(1,128)S(1)} %get-tuple-element.262.prior_ref.refs_5_.refs_7_.refs_9_.refs_11_), custom_call_target="tpu_custom_call" | custom-call | flops 20000000000 | bytes 311296 | tf_op jit(solution)/shard_map/cond/branch_0_fun/factor_inverse/pallas_call | solution.py:105
  269.5 4.1 right_side.8.refs_1_
  273.6 2.5 right_side.9.refs_1_
  276.1 2.4 right_side.10.refs_2_
  278.5 3.7 right_side.11.refs_2_.refs_4_.refs_6_.refs_8_
  282.2 0.5 collective-permute-start.2
  282.7 27.9 %tiles.8 = (f32[8,768,3072]{2,1,0:T(8,128)}, f32[8,768,128]{2,1,0:T(8,128)}) custom-call(s32[5]{0:T(128)S(1)} %stack.40.at_ref, s32[4]{0:T(128)S(1)} %broadcast_xor_fusion.order_ref, bf16[1216,768]{1,0:T(8,128)(2,1)} %whiten.2.refs_0_, bf16[1216,768]{1,0:T(8,128)(2,1)} %collective-permute-done.16.refs_1_, ...), custom_call_target="tpu_custom_call" | custom-call | flops 15703474176 | bytes 29097984 | tf_op jit(solution)/shard_map/cond/branch_0_fun/tiles/pallas_call | solution.py:227
  310.7 0.1 collective-permute-start.9
  310.8 0.4 collective-permute-start.4
  311.2 26.6 %tiles.9 = (f32[8,768,3072]{2,1,0:T(8,128)}, f32[8,768,128]{2,1,0:T(8,128)}) custom-call(s32[5]{0:T(128)S(1)} %stack.38.at_ref, s32[4]{0:T(128)S(1)} %broadcast_xor_fusion.order_ref, bf16[1216,768]{1,0:T(8,128)(2,1)} %collective-permute-done.refs_0_, ...), custom_call_target="tpu_custom_call", output_to_operand_aliasing={{0}: (11, {}), {1}: (12, {})} | custom-call | flops 15703474176 | bytes 29097984 | tf_op jit(solution)/shard_map/cond/branch_0_fun/tiles/pallas_call | solution.py:227
  337.9 1.2 copy-done.15
  339.1 28.1 %tiles.10 = (f32[8,768,3072]{2,1,0:T(8,128)}, f32[8,768,128]{2,1,0:T(8,128)}) custom-call(s32[5]{0:T(128)S(1)} %stack.37.at_ref, s32[4]{0:T(128)S(1)} %broadcast_xor_fusion.order_ref, bf16[1216,768]{1,0:T(8,128)(2,1)} %collective-permute-done.1.refs_0_, ...), custom_call_target="tpu_custom_call", output_to_operand_aliasing={{0}: (13, {}), {1}: (14, {})} | custom-call | flops 15703474176 | bytes 29097984 | tf_op jit(solution)/shard_map/cond/branch_0_fun/tiles/pallas_call | solution.py:227
  367.2 1.2 copy-done.17
  368.4 0.6 copy-done.18
  369.0 27.9 %tiles.11 = (f32[8,768,3072]{2,1,0:T(8,128)}, f32[8,768,128]{2,1,0:T(8,128)}) custom-call(s32[5]{0:T(128)S(1)} %stack.36.at_ref, s32[4]{0:T(128)S(1)} %broadcast_xor_fusion.order_ref, bf16[1216,768]{1,0:T(8,128)(2,1)} %collective-permute-done.1.refs_0_, ...), custom_call_target="tpu_custom_call", output_to_operand_aliasing={{0}: (15, {}), {1}: (16, {})} | custom-call | flops 15703474176 | bytes 29097984 | tf_op jit(solution)/shard_map/cond/branch_0_fun/tiles/pallas_call | solution.py:227
  (58 shorter events, 0.3 us)
Async XLA Ops:
  7.2 6.4 %copy-start.20 = (s32[4]{0:T(128)S(1)}, s32[4]{0:T(128)}, u32[]{:S(2)}) copy-start(s32[4]{0:T(128)} %param.21) | copy-start | bytes 52
  7.2 6.4 %copy-start.19 = (s32[4,512]{1,0:T(4,128)S(1)}, s32[4,512]{1,0:T(4,128)}, u32[]{:S(2)}) copy-start(s32[4,512]{1,0:T(4,128)} %param.22) | copy-start | bytes 24580
  9.0 21.5 %collective-permute-start.34 = (bf16[512,768]{1,0:T(8,128)(2,1)S(1)}, bf16[512,768]{1,0:T(8,128)(2,1)}, u32[]{:S(2)}, u32[]{:S(2)}) collective-permute-start(bf16[512,768]{1,0:T(8,128)(2,1)S(1)} %get-tuple-element.267), channel_id=1, source_target_pairs={{0,8},{8,0},{16,24},{24,16},{1,9},{9,1},{17,25},{25,17},{2,10},{10... | collective-permute-start | bytes 2359304 | tf_op jit(solution)/shard_map/ppermute | solution.py:356
  12.0 36.0 %collective-permute-start.35 = (bf16[512,768]{1,0:T(8,128)(2,1)S(1)}, bf16[512,768]{1,0:T(8,128)(2,1)}, u32[]{:S(2)}, u32[]{:S(2)}) collective-permute-start(bf16[512,768]{1,0:T(8,128)(2,1)S(1)} %get-tuple-element.268), channel_id=1, source_target_pairs={{0,16},{8,24},{16,0},{24,8},{1,17},{9,25},{17,1},{25,9},{2,18},{10... | collective-permute-start | bytes 2359304 | tf_op jit(solution)/shard_map/ppermute | solution.py:356
  13.5 34.4 %collective-permute-start.36 = (bf16[512,768]{1,0:T(8,128)(2,1)S(1)}, bf16[512,768]{1,0:T(8,128)(2,1)}, u32[]{:S(2)}, u32[]{:S(2)}) collective-permute-start(bf16[512,768]{1,0:T(8,128)(2,1)S(1)} %get-tuple-element.266), channel_id=1, source_target_pairs={{0,24},{8,16},{16,8},{24,0},{1,25},{9,17},{17,9},{25,1},{2,26},{10... | collective-permute-start | bytes 2359304 | tf_op jit(solution)/shard_map/ppermute | solution.py:356
  48.0 203.8 %all-reduce.4.cloned.1.call-start = ((), (), s32[]{:S(2)}) async-start(), calls=%async_computation | async-start | bytes 622592 | tf_op jit(solution)/shard_map/cond/branch_0_fun/psum | solution.py:384
  64.5 60.6 %copy-start.27 = (s32[4]{0:T(128)S(1)}, s32[4]{0:T(128)}, u32[]{:S(2)}) copy-start(s32[4]{0:T(128)} %constant.107.clone.1) | copy-start | bytes 52 | tf_op jit(solution)/shard_map/cond
  64.5 61.2 %copy-start.26 = (s32[4]{0:T(128)S(1)}, s32[4]{0:T(128)}, u32[]{:S(2)}) copy-start(s32[4]{0:T(128)} %constant.108.clone.1) | copy-start | bytes 52 | tf_op jit(solution)/shard_map/cond
  64.5 61.8 %copy-start.25 = (s32[4]{0:T(128)S(1)}, s32[4]{0:T(128)}, u32[]{:S(2)}) copy-start(s32[4]{0:T(128)} %constant.109.clone.1) | copy-start | bytes 52 | tf_op jit(solution)/shard_map/cond
  64.5 62.4 %copy-start.24 = (s32[4]{0:T(128)S(1)}, s32[4]{0:T(128)}, u32[]{:S(2)}) copy-start(s32[4]{0:T(128)} %constant.110.clone.1) | copy-start | bytes 52 | tf_op jit(solution)/shard_map/cond
  64.5 63.0 %copy-start.23 = (s32[4]{0:T(128)S(1)}, s32[4]{0:T(128)}, u32[]{:S(2)}) copy-start(s32[4]{0:T(128)} %constant.111.clone.1) | copy-start | bytes 52 | tf_op jit(solution)/shard_map/cond
  64.5 63.6 %copy-start.22 = (s32[4]{0:T(128)S(1)}, s32[4]{0:T(128)}, u32[]{:S(2)}) copy-start(s32[4]{0:T(128)} %constant.112.clone.1) | copy-start | bytes 52 | tf_op jit(solution)/shard_map/cond
  64.5 43.6 %collective-permute-start.5 = (bf16[1216,768]{1,0:T(8,128)(2,1)}, bf16[1216,768]{1,0:T(8,128)(2,1)S(1)}, u32[]{:S(2)}, u32[]{:S(2)}) collective-permute-start(bf16[1216,768]{1,0:T(8,128)(2,1)} %whiten.2.refs_0_), channel_id=1, source_target_pairs={{2,0},{3,1},{4,2},{5,3},{6,4},{7,5},{10,8},{11,9},{12,10},{13,11},... | collective-permute-start | bytes 5603336 | tf_op jit(solution)/shard_map/cond/branch_0_fun/ppermute | solution.py:363
  66.0 43.4 %collective-permute-start = (bf16[1216,768]{1,0:T(8,128)(2,1)}, bf16[1216,768]{1,0:T(8,128)(2,1)}, u32[]{:S(2)}, u32[]{:S(2)}) collective-permute-start(bf16[1216,768]{1,0:T(8,128)(2,1)} %whiten.2.refs_0_), channel_id=1, source_target_pairs={{0,2},{1,3},{2,4},{3,5},{4,6},{5,7},{8,10},{9,11},{10,12},{11,13},... | collective-permute-start | bytes 5603336 | tf_op jit(solution)/shard_map/cond/branch_0_fun/ppermute | solution.py:363
  71.8 43.5 %collective-permute-start.10 = (bf16[1216,768]{1,0:T(8,128)(2,1)}, bf16[1216,768]{1,0:T(8,128)(2,1)S(1)}, u32[]{:S(2)}, u32[]{:S(2)}) collective-permute-start(bf16[1216,768]{1,0:T(8,128)(2,1)} %whiten.2.refs_0_), channel_id=1, source_target_pairs={{0,16},{8,24},{16,0},{24,8},{1,17},{9,25},{17,1},{25,9},{2,18},{10... | collective-permute-start | bytes 5603336 | tf_op jit(solution)/shard_map/cond/branch_0_fun/ppermute | solution.py:356
  73.3 45.6 %collective-permute-start.12 = (bf16[1216,768]{1,0:T(8,128)(2,1)}, bf16[1216,768]{1,0:T(8,128)(2,1)S(1)}, u32[]{:S(2)}, u32[]{:S(2)}) collective-permute-start(bf16[1216,768]{1,0:T(8,128)(2,1)} %whiten.2.refs_0_), channel_id=1, source_target_pairs={{0,8},{8,0},{16,24},{24,16},{1,9},{9,1},{17,25},{25,17},{2,10},{10... | collective-permute-start | bytes 5603336 | tf_op jit(solution)/shard_map/cond/branch_0_fun/ppermute | solution.py:356
  108.1 44.2 %collective-permute-start.6 = (bf16[1216,768]{1,0:T(8,128)(2,1)S(1)}, bf16[1216,768]{1,0:T(8,128)(2,1)}, u32[]{:S(2)}, u32[]{:S(2)}) collective-permute-start(bf16[1216,768]{1,0:T(8,128)(2,1)S(1)} %collective-permute-done.5.refs_2_), channel_id=1, source_target_pairs={{2,0},{3,1},{4,2},{5,3},{6,4},{7,5},{10,8},{11,9},{12,10},{13,11},... | collective-permute-start | bytes 5603336 | tf_op jit(solution)/shard_map/cond/branch_0_fun/ppermute | solution.py:363
  109.4 44.2 %collective-permute-start.1 = (bf16[1216,768]{1,0:T(8,128)(2,1)}, bf16[1216,768]{1,0:T(8,128)(2,1)}, u32[]{:S(2)}, u32[]{:S(2)}) collective-permute-start(bf16[1216,768]{1,0:T(8,128)(2,1)} %collective-permute-done.refs_0_), channel_id=1, source_target_pairs={{0,2},{1,3},{2,4},{3,5},{4,6},{5,7},{8,10},{9,11},{10,12},{11,13},... | collective-permute-start | bytes 5603336 | tf_op jit(solution)/shard_map/cond/branch_0_fun/ppermute | solution.py:363
  116.3 1.2 copy-start.8
  117.5 20.6 %collective-permute-start.11 = (bf16[608,768]{1,0:T(8,128)(2,1)}, bf16[608,768]{1,0:T(8,128)(2,1)S(1)}, u32[]{:S(2)}, u32[]{:S(2)}) collective-permute-start(bf16[608,768]{1,0:T(8,128)(2,1)} %slice.41), channel_id=1, source_target_pairs={{0,8},{8,0},{16,24},{24,16},{1,9},{9,1},{17,25},{25,17},{2,10},{10... | collective-permute-start | bytes 2801672 | tf_op jit(solution)/shard_map/cond/branch_0_fun/ppermute | solution.py:356
  119.9 1.2 copy-start.10
  121.2 20.8 %collective-permute-start.13 = (bf16[608,768]{1,0:T(8,128)(2,1)}, bf16[608,768]{1,0:T(8,128)(2,1)}, u32[]{:S(2)}, u32[]{:S(2)}) collective-permute-start(bf16[608,768]{1,0:T(8,128)(2,1)} %slice.42), channel_id=1, source_target_pairs={{0,16},{8,24},{16,0},{24,8},{1,17},{9,25},{17,1},{25,9},{2,18},{10... | collective-permute-start | bytes 2801672 | tf_op jit(solution)/shard_map/cond/branch_0_fun/ppermute | solution.py:356
  121.7 160.5 %collective-permute-start.16 = (bf16[1216,768]{1,0:T(8,128)(2,1)}, bf16[1216,768]{1,0:T(8,128)(2,1)}, u32[]{:S(2)}, u32[]{:S(2)}) collective-permute-start(bf16[1216,768]{1,0:T(8,128)(2,1)} %whiten.2.refs_0_), channel_id=1, source_target_pairs={{0,1},{1,0},{2,3},{3,2},{4,5},{5,4},{6,7},{7,6},{8,9},{9,8},{10,11... | collective-permute-start | bytes 5603336 | tf_op jit(solution)/shard_map/cond/branch_0_fun/ppermute | solution.py:359
  138.1 144.1 %collective-permute-start.14 = (bf16[1216,768]{1,0:T(8,128)(2,1)S(1)}, bf16[1216,768]{1,0:T(8,128)(2,1)}, u32[]{:S(2)}, u32[]{:S(2)}) collective-permute-start(bf16[1216,768]{1,0:T(8,128)(2,1)S(1)} %collective-permute-done.5.refs_2_), channel_id=1, source_target_pairs={{0,1},{1,0},{2,3},{3,2},{4,5},{5,4},{6,7},{7,6},{8,9},{9,8},{10,11... | collective-permute-start | bytes 5603336 | tf_op jit(solution)/shard_map/cond/branch_0_fun/ppermute | solution.py:359
  142.0 169.3 %collective-permute-start.15 = (bf16[1216,768]{1,0:T(8,128)(2,1)}, bf16[1216,768]{1,0:T(8,128)(2,1)}, u32[]{:S(2)}, u32[]{:S(2)}) collective-permute-start(bf16[1216,768]{1,0:T(8,128)(2,1)} %collective-permute-done.refs_0_), channel_id=1, source_target_pairs={{0,1},{1,0},{2,3},{3,2},{4,5},{5,4},{6,7},{7,6},{8,9},{9,8},{10,11... | collective-permute-start | bytes 5603336 | tf_op jit(solution)/shard_map/cond/branch_0_fun/ppermute | solution.py:359
  152.3 158.3 %collective-permute-start.8 = (bf16[1216,768]{1,0:T(8,128)(2,1)}, bf16[1216,768]{1,0:T(8,128)(2,1)}, u32[]{:S(2)}, u32[]{:S(2)}) collective-permute-start(bf16[1216,768]{1,0:T(8,128)(2,1)} %collective-permute-done.6.refs_4_), channel_id=1, source_target_pairs={{2,0},{3,1},{4,2},{5,3},{6,4},{7,5},{10,8},{11,9},{12,10},{13,11},... | collective-permute-start | bytes 5603336 | tf_op jit(solution)/shard_map/cond/branch_0_fun/ppermute | solution.py:363
  153.7 157.1 %collective-permute-start.3 = (bf16[1216,768]{1,0:T(8,128)(2,1)}, bf16[1216,768]{1,0:T(8,128)(2,1)}, u32[]{:S(2)}, u32[]{:S(2)}) collective-permute-start(bf16[1216,768]{1,0:T(8,128)(2,1)} %collective-permute-done.1.refs_0_), channel_id=1, source_target_pairs={{0,2},{1,3},{2,4},{3,5},{4,6},{5,7},{8,10},{9,11},{10,12},{11,13},... | collective-permute-start | bytes 5603336 | tf_op jit(solution)/shard_map/cond/branch_0_fun/ppermute | solution.py:363
  251.7 1.0 copy-start.2
  252.7 16.8 %copy-start.3 = (bf16[1216,128]{1,0:T(8,128)(2,1)S(1)}, bf16[1216,128]{1,0:T(8,128)(2,1)}, u32[]{:S(2)}) copy-start(bf16[1216,128]{1,0:T(8,128)(2,1)} %all-reduce.4.cloned.1.call-done.first_ref) | copy-start | bytes 933892 | tf_op jit(solution)/shard_map/cond
  269.5 4.1 copy-start.11
  273.6 2.5 copy-start.9
  282.2 55.6 %collective-permute-start.7 = (bf16[1216,768]{1,0:T(8,128)(2,1)}, bf16[1216,768]{1,0:T(8,128)(2,1)S(1)}, u32[]{:S(2)}, u32[]{:S(2)}) collective-permute-start(bf16[1216,768]{1,0:T(8,128)(2,1)} %collective-permute-done.6.refs_4_), channel_id=1, source_target_pairs={{0,1},{1,0},{2,3},{3,2},{4,5},{5,4},{6,7},{7,6},{8,9},{9,8},{10,11... | collective-permute-start | bytes 5603336 | tf_op jit(solution)/shard_map/cond/branch_0_fun/ppermute | solution.py:359
  282.2 55.6 %collective-permute-start.2 = (bf16[1216,768]{1,0:T(8,128)(2,1)}, bf16[1216,768]{1,0:T(8,128)(2,1)S(1)}, u32[]{:S(2)}, u32[]{:S(2)}) collective-permute-start(bf16[1216,768]{1,0:T(8,128)(2,1)} %collective-permute-done.1.refs_0_), channel_id=1, source_target_pairs={{0,1},{1,0},{2,3},{3,2},{4,5},{5,4},{6,7},{7,6},{8,9},{9,8},{10,11... | collective-permute-start | bytes 5603336 | tf_op jit(solution)/shard_map/cond/branch_0_fun/ppermute | solution.py:359
  310.7 56.5 %collective-permute-start.9 = (bf16[1216,768]{1,0:T(8,128)(2,1)}, bf16[1216,768]{1,0:T(8,128)(2,1)S(1)}, u32[]{:S(2)}, u32[]{:S(2)}) collective-permute-start(bf16[1216,768]{1,0:T(8,128)(2,1)} %collective-permute-done.8.refs_6_), channel_id=1, source_target_pairs={{0,1},{1,0},{2,3},{3,2},{4,5},{5,4},{6,7},{7,6},{8,9},{9,8},{10,11... | collective-permute-start | bytes 5603336 | tf_op jit(solution)/shard_map/cond/branch_0_fun/ppermute | solution.py:359
  310.8 56.4 %collective-permute-start.4 = (bf16[1216,768]{1,0:T(8,128)(2,1)}, bf16[1216,768]{1,0:T(8,128)(2,1)S(1)}, u32[]{:S(2)}, u32[]{:S(2)}) collective-permute-start(bf16[1216,768]{1,0:T(8,128)(2,1)} %collective-permute-done.3.refs_2_), channel_id=1, source_target_pairs={{0,1},{1,0},{2,3},{3,2},{4,5},{5,4},{6,7},{7,6},{8,9},{9,8},{10,11... | collective-permute-start | bytes 5603336 | tf_op jit(solution)/shard_map/cond/branch_0_fun/ppermute | solution.py:359
  337.8 1.3 copy-start.15
  367.2 1.2 copy-start.17
  367.2 1.8 copy-start.18
Sparse Core Ops, SparseCore 0:
  123.6 128.1 all-reduce.3

commit v2 on v1

--- a/solution.py
+++ b/solution.py
@@ -369,19 +369,23 @@
     for s in range(1, rows):
         raw.append(swap_row(strip_of(row_index ^ s), s))
 
+    begin = design[:, :PANEL]
+    begin = jnp.where(col_index == 1, swap_core(begin), begin)
+    for t in range(1, chips):
+        begin = jnp.where(chip == t, shift(begin, 1), begin)
+    raw_first = [begin] + [swap_row(begin, s) for s in range(1, rows)]
+
     column_prior = lax.dynamic_slice_in_dim(
         prior_diag, col_index * col_width + row_index * width, width
     ).reshape(1, width)
     first_prior = prior_diag[:PANEL]
     table = line_schedule(chips)
 
-    def run(sent, raw):
+    def run(sent, raw, raw_first):
         kept = -(-sent // LANES) * LANES
-        own = whiten(order, compact_whitener(whitener, live, sent), raw)
-
-        mine = (row_index == 0) & (col_index == 0)
-        first = jnp.where(mine, own[:, :PANEL], jnp.zeros((sent, PANEL), BF16))
-        first = lax.psum(first, ("row", "col"))
+        mixer = compact_whitener(whitener, live, sent)
+        own = whiten(order, mixer, raw)
+        first = whiten(order, mixer, raw_first)
 
         moving = {0: own, 1: own}
         arrived = {}
@@ -437,6 +441,7 @@
         jnp.where(count <= sizes[0], 0, 1),
         [functools.partial(run, size) for size in sizes],
         raw,
+        raw_first,
     )
 
 

time: 420 us -> 341 us (0.81)
  waiting for transfers between devices: 179 us -> 91.8 us
  starting transfers between devices: 31.6 us -> 51.3 us
  between operations: 15 us -> 2.44 us
    psum x1 -> x0, waiting for transfers between devices: 91.7 us -> none  [run(): first = lax.psum(first, ('row', 'col'))]
    ppermute x6 -> x9, starting transfers between devices: 22 us -> 34.5 us  [shift(): return lax.ppermute(value, 'col', pairs)]
    ppermute x7 -> x10, starting transfers between devices: 8.51 us -> 15.2 us  [swap_row(): return lax.ppermute(value, 'row', [(r, r ^ mask) for r in range(rows)])]
    ppermute x6 -> x9, waiting for transfers between devices: 44.7 us -> 50.3 us  [shift(): return lax.ppermute(value, 'col', pairs)]
    pallas_call x1 -> x2, Pallas kernels: 8.14 us -> 11.7 us  [whiten(): pl.pallas_call(whiten_kernel, grid_spec=pltpu.PrefetchScalarGridSpec(num_...]
    ppermute x7 -> x10, waiting for transfers between devices: 42.4 us -> 40.5 us  [swap_row(): return lax.ppermute(value, 'row', [(r, r ^ mask) for r in range(rows)])]
  transfers between devices with their start and end apart: 21 -> 27, of which waited for: 7 -> 10; matrix products, arithmetic and copies ran while one was open for 3% -> 4% of each run, Pallas kernels for 27% -> 34%
where the time goes in v2:
time: 341 us; the launch traced here: 335 us
  Pallas kernels  150 us (44%)
  waiting for transfers between devices  91.8 us (27%)
  starting transfers between devices  51.3 us (15%)
  local copies, waits for them, and re-layouts  21.1 us (6%)
  loops' own time  8.99 us (3%)
  matrix products  6.04 us (2%)
    pallas_call x4, Pallas kernels, tiles(): pl.pallas_call(functools.partial(tile_kernel, kept, len(pairs)), grid_spe...  110 us
    ppermute x9, waiting for transfers between devices, shift(): return lax.ppermute(value, 'col', pairs)  50.3 us
    ppermute x10, waiting for transfers between devices, swap_row(): return lax.ppermute(value, 'row', [(r, r ^ mask) for r in range(rows)])  40.5 us
    ppermute x9, starting transfers between devices, shift(): return lax.ppermute(value, 'col', pairs)  34.5 us
    pallas_call x1, Pallas kernels, factor_inverse(): pl.pallas_call(factor_kernel, out_shape=(square, square), compiler_params...  16.8 us
    ppermute x10, starting transfers between devices, swap_row(): return lax.ppermute(value, 'row', [(r, r ^ mask) for r in range(rows)])  15.2 us
    pallas_call x2, Pallas kernels, whiten(): pl.pallas_call(whiten_kernel, grid_spec=pltpu.PrefetchScalarGridSpec(num_...  11.7 us
    pallas_call x4, Pallas kernels, right_side(): pl.pallas_call(functools.partial(right_kernel, kept, len(parts)), grid_sp...  11.5 us
  transfers between devices with their start and end apart: 27, of which 10 were waited for; matrix products, arithmetic and copies ran while one was open for 4% of the time, Pallas kernels for 34%

profile of v2, /device:TPU:0, one launch (start us, length us, event | category | flops | bytes accessed | tf_op | source)
XLA Modules:
  0.0 334.9 jit_solution(2749774376112141255)
XLA Ops:
  0.6 0.9 slice.32
  2.1 1.0 collective-permute-done.37
  3.1 0.9 broadcast_select_fusion
  4.0 4.8 %collective-permute-start.38 = (bf16[512,128]{1,0:T(8,128)(2,1)S(1)}, bf16[512,128]{1,0:T(8,128)(2,1)S(1)}, u32[]{:S(2)}, u32[]{:S(2)}) collective-permute-start(bf16[512,128]{1,0:T(8,128)(2,1)S(1)} %broadcast_select_fusion), channel_id=1, source_target_pairs={{0,2},{1,3},{2,4},{3,5},{4,6},{5,7},{8,10},{9,11},{10,12},{11,13},... | collective-permute-start | bytes 393224 | tf_op jit(solution)/shard_map/ppermute | solution.py:363
  8.9 3.0 collective-permute-done.38
  11.9 4.4 %collective-permute-start.39 = (bf16[512,128]{1,0:T(8,128)(2,1)S(1)}, bf16[512,128]{1,0:T(8,128)(2,1)S(1)}, u32[]{:S(2)}, u32[]{:S(2)}) collective-permute-start(bf16[512,128]{1,0:T(8,128)(2,1)S(1)} %broadcast_select_fusion.1), channel_id=1, source_target_pairs={{0,2},{1,3},{2,4},{3,5},{4,6},{5,7},{8,10},{9,11},{10,12},{11,13},... | collective-permute-start | bytes 393224 | tf_op jit(solution)/shard_map/ppermute | solution.py:363
  16.3 3.1 constant_dynamic-slice_fusion.4
  19.4 1.5 collective-permute-start.34
  20.9 1.5 collective-permute-start.35
  22.9 3.5 %collective-permute-start.40 = (bf16[512,128]{1,0:T(8,128)(2,1)S(1)}, bf16[512,128]{1,0:T(8,128)(2,1)S(1)}, u32[]{:S(2)}, u32[]{:S(2)}) collective-permute-start(bf16[512,128]{1,0:T(8,128)(2,1)S(1)} %broadcast_select_fusion.2), channel_id=1, source_target_pairs={{0,2},{1,3},{2,4},{3,5},{4,6},{5,7},{8,10},{9,11},{10,12},{11,13},... | collective-permute-start | bytes 393224 | tf_op jit(solution)/shard_map/ppermute | solution.py:363
  26.4 2.5 collective-permute-done.40
  28.9 1.6 collective-permute-start.41
  30.5 1.5 collective-permute-start.42
  32.0 25.8 %collective-permute-done.41 = bf16[512,128]{1,0:T(8,128)(2,1)S(1)} collective-permute-done((bf16[512,128]{1,0:T(8,128)(2,1)S(1)}, bf16[512,128]{1,0:T(8,128)(2,1)S(1)}, u32[]{:S(2)}, u32[]{:S(2)}) %collective-permute-start.41) | collective-permute-done | bytes 131104 | tf_op jit(solution)/shard_map/ppermute | solution.py:356
  57.8 2.4 collective-permute-start.43
  60.3 0.7 convert_reduce_fusion
  61.5 2.3 collective-permute-done.43
  63.8 0.6 iota.19
  64.4 269.3 %conditional.1 = ((f32[8,768,3072]{2,1,0:T(8,128)}, f32[8,768,128]{2,1,0:T(8,128)})) conditional(s32[]{:T(128)} %clamp.3, (s32[]{:T(128)}, (), s32[]{:T(128)}, s32[]{:T(128)}, (), /*index=5*/pred[4,512]{1,0:T(4,128)(4,1)S(1)}, bf16[4,512,512]{2,1,0:T(8,128)(2,1)}, s32[]{:T(128)}, bf16[512,3072]{1,0:T(8,128)(2,1)S(1)}, bf16[512,768]{1,0:T(8,128)(2,1)}, ...), branch_computations={%region_1.4_spmd, %region_4.7_spmd} | conditional | flops 103160733696 | bytes 404223264 | solution.py:440
  65.3 0.7 slice.36
  66.0 0.6 reshape.107
  66.6 0.7 reduce-window.13
  67.6 0.7 fusion.7
  68.3 6.0 %select_convert_fusion.mixer_ref = bf16[4,1216,512]{2,1,0:T(8,128)(2,1)} fusion(bf16[4,512,512]{2,1,0:T(8,128)(2,1)} %get-tuple-element.188, s32[4,512]{1,0:T(4,128)S(1)} %fusion.7, pred[4,512]{1,0:T(4,128)(4,1)} %copy-done.22), kind=kOutput, calls=%fused_computation | convolution fusion | flops 2560098304 | bytes 7088128 | tf_op jit(solution)/shard_map/cond/branch_0_fun/ake,aef->akf/dot_general | solution.py:44
  74.9 8.4 %whiten.4.refs_0_ = bf16[1216,768]{1,0:T(8,128)(2,1)} custom-call(s32[4]{0:T(128)S(1)} %broadcast_xor_fusion.order_ref, bf16[4,1216,512]{2,1,0:T(8,128)(2,1)} %select_convert_fusion.mixer_ref, bf16[512,768]{1,0:T(8,128)(2,1)S(1)} %constant_dynamic-slice_fusion.refs_0_, bf16[512,768]{1,0:T(8,128)(2,1)} %get-tuple-element.97.refs_1_, ...), custom_call_target="tpu_custom_call" | custom-call | flops 3825205248 | bytes 8126464 | tf_op jit(solution)/shard_map/cond/branch_0_fun/whiten/pallas_call | solution.py:60
  83.2 1.3 collective-permute-start.5
  84.5 5.8 %collective-permute-start = (bf16[1216,768]{1,0:T(8,128)(2,1)}, bf16[1216,768]{1,0:T(8,128)(2,1)}, u32[]{:S(2)}, u32[]{:S(2)}) collective-permute-start(bf16[1216,768]{1,0:T(8,128)(2,1)} %whiten.4.refs_0_), channel_id=1, source_target_pairs={{0,2},{1,3},{2,4},{3,5},{4,6},{5,7},{8,10},{9,11},{10,12},{11,13},... | collective-permute-start | bytes 5603336 | tf_op jit(solution)/shard_map/cond/branch_0_fun/ppermute | solution.py:363
  90.3 1.5 collective-permute-start.10
  91.9 1.5 collective-permute-start.12
  93.4 31.7 %collective-permute-done.5.refs_2_ = bf16[1216,768]{1,0:T(8,128)(2,1)S(1)} collective-permute-done((bf16[1216,768]{1,0:T(8,128)(2,1)}, bf16[1216,768]{1,0:T(8,128)(2,1)S(1)}, u32[]{:S(2)}, u32[]{:S(2)}) %collective-permute-start.5) | collective-permute-done | bytes 1867808 | tf_op jit(solution)/shard_map/cond/branch_0_fun/ppermute | solution.py:363
  125.0 1.3 collective-permute-start.6
  126.3 5.9 %collective-permute-start.1 = (bf16[1216,768]{1,0:T(8,128)(2,1)}, bf16[1216,768]{1,0:T(8,128)(2,1)}, u32[]{:S(2)}, u32[]{:S(2)}) collective-permute-start(bf16[1216,768]{1,0:T(8,128)(2,1)} %collective-permute-done.refs_0_), channel_id=1, source_target_pairs={{0,2},{1,3},{2,4},{3,5},{4,6},{5,7},{8,10},{9,11},{10,12},{11,13},... | collective-permute-start | bytes 5603336 | tf_op jit(solution)/shard_map/cond/branch_0_fun/ppermute | solution.py:363
  132.3 1.6 collective-permute-start.11
  133.9 1.6 collective-permute-start.13
  135.5 3.3 whiten.5.first_ref
  138.8 0.7 slice_bitcast_fusion
  139.5 11.4 %collective-permute-done.11.refs_0_ = bf16[608,768]{1,0:T(8,128)(2,1)S(1)} collective-permute-done((bf16[608,768]{1,0:T(8,128)(2,1)S(1)}, bf16[608,768]{1,0:T(8,128)(2,1)S(1)}, u32[]{:S(2)}, u32[]{:S(2)}) %collective-permute-start.11) | collective-permute-done | bytes 933920 | tf_op jit(solution)/shard_map/cond/branch_0_fun/ppermute | solution.py:356
  151.0 1.0 collective-permute-done.13.refs_1_
  151.9 0.9 copy-done.14
  152.9 12.9 %collective-permute-done.6.refs_4_ = bf16[1216,768]{1,0:T(8,128)(2,1)} collective-permute-done((bf16[1216,768]{1,0:T(8,128)(2,1)S(1)}, bf16[1216,768]{1,0:T(8,128)(2,1)}, u32[]{:S(2)}, u32[]{:S(2)}) %collective-permute-start.6) | collective-permute-done | bytes 1867808 | tf_op jit(solution)/shard_map/cond/branch_0_fun/ppermute | solution.py:363
  165.8 1.3 collective-permute-start.8
  167.3 6.2 %collective-permute-start.3 = (bf16[1216,768]{1,0:T(8,128)(2,1)}, bf16[1216,768]{1,0:T(8,128)(2,1)}, u32[]{:S(2)}, u32[]{:S(2)}) collective-permute-start(bf16[1216,768]{1,0:T(8,128)(2,1)} %collective-permute-done.1.refs_0_), channel_id=1, source_target_pairs={{0,2},{1,3},{2,4},{3,5},{4,6},{5,7},{8,10},{9,11},{10,12},{11,13},... | collective-permute-start | bytes 5603336 | tf_op jit(solution)/shard_map/cond/branch_0_fun/ppermute | solution.py:363
  173.6 16.8 %factor_inverse.2 = (f32[128,128]{1,0:T(8,128)S(1)}, f32[128,128]{1,0:T(8,128)S(1)}) custom-call(bf16[1216,128]{1,0:T(8,128)(2,1)S(1)} %whiten.5.first_ref, f32[1,128]{1,0:T(1,128)S(1)} %get-tuple-element.242.prior_ref.refs_5_.refs_7_.refs_9_.refs_11_), custom_call_target="tpu_custom_call" | custom-call | flops 20000000000 | bytes 311296 | tf_op jit(solution)/shard_map/cond/branch_0_fun/factor_inverse/pallas_call | solution.py:105
  190.5 0.8 dynamic_slice.58
  191.3 0.6 dynamic_slice.38
  191.9 0.6 dynamic_slice.39
  192.5 0.6 dynamic_slice.36
  193.2 0.7 dynamic_slice.37
  193.8 0.7 dynamic_slice.34
  194.5 0.6 dynamic_slice.35
  195.2 1.3 stack.38.at_ref
  196.6 1.4 stack.37.at_ref
  198.0 1.4 stack.36.at_ref
  199.3 4.1 %right_side.8.refs_1_ = bf16[4,1664,768]{2,1,0:T(8,128)(2,1)} custom-call(s32[1]{0:T(128)} %bitcast.8.where_ref, bf16[1216,128]{1,0:T(8,128)(2,1)S(1)} %whiten.5.first_ref, f32[128,1]{1,0:T(8,128)S(1)} %copy.66.prior_ref, f32[128,128]{1,0:T(8,128)S(1)} %get-tuple-element.105.inv_ref, bf16[1216,768]{1,0:T(8,128)(2,1)} %whiten.4.refs_0_), custom_call_target="tpu_custom_call" | custom-call | flops 402653184 | bytes 5111808 | tf_op jit(solution)/shard_map/cond/branch_0_fun/right_side/pallas_call | solution.py:144
  203.4 2.4 right_side.9.refs_1_
  205.8 2.5 right_side.10.refs_2_
  208.3 2.5 right_side.11.refs_2_.refs_4_.refs_6_.refs_8_
  211.3 27.8 %tiles.8 = (f32[8,768,3072]{2,1,0:T(8,128)}, f32[8,768,128]{2,1,0:T(8,128)}) custom-call(s32[5]{0:T(128)S(1)} %stack.40.at_ref, s32[4]{0:T(128)S(1)} %broadcast_xor_fusion.order_ref, bf16[1216,768]{1,0:T(8,128)(2,1)} %whiten.4.refs_0_, bf16[1216,768]{1,0:T(8,128)(2,1)} %collective-permute-done.16.refs_1_, ...), custom_call_target="tpu_custom_call" | custom-call | flops 15703474176 | bytes 29097984 | tf_op jit(solution)/shard_map/cond/branch_0_fun/tiles/pallas_call | solution.py:227
  239.8 26.5 %tiles.9 = (f32[8,768,3072]{2,1,0:T(8,128)}, f32[8,768,128]{2,1,0:T(8,128)}) custom-call(s32[5]{0:T(128)S(1)} %stack.38.at_ref, s32[4]{0:T(128)S(1)} %broadcast_xor_fusion.order_ref, bf16[1216,768]{1,0:T(8,128)(2,1)} %collective-permute-done.refs_0_, ...), custom_call_target="tpu_custom_call", output_to_operand_aliasing={{0}: (11, {}), {1}: (12, {})} | custom-call | flops 15703474176 | bytes 29097984 | tf_op jit(solution)/shard_map/cond/branch_0_fun/tiles/pallas_call | solution.py:227
  266.3 1.2 copy-done.17
  267.5 28.0 %tiles.10 = (f32[8,768,3072]{2,1,0:T(8,128)}, f32[8,768,128]{2,1,0:T(8,128)}) custom-call(s32[5]{0:T(128)S(1)} %stack.37.at_ref, s32[4]{0:T(128)S(1)} %broadcast_xor_fusion.order_ref, bf16[1216,768]{1,0:T(8,128)(2,1)} %collective-permute-done.1.refs_0_, ...), custom_call_target="tpu_custom_call", output_to_operand_aliasing={{0}: (13, {}), {1}: (14, {})} | custom-call | flops 15703474176 | bytes 29097984 | tf_op jit(solution)/shard_map/cond/branch_0_fun/tiles/pallas_call | solution.py:227
  295.5 1.2 copy-done.20
  296.7 0.6 copy-done.21
  297.3 27.8 %tiles.11 = (f32[8,768,3072]{2,1,0:T(8,128)}, f32[8,768,128]{2,1,0:T(8,128)}) custom-call(s32[5]{0:T(128)S(1)} %stack.36.at_ref, s32[4]{0:T(128)S(1)} %broadcast_xor_fusion.order_ref, bf16[1216,768]{1,0:T(8,128)(2,1)} %collective-permute-done.1.refs_0_, ...), custom_call_target="tpu_custom_call", output_to_operand_aliasing={{0}: (15, {}), {1}: (16, {})} | custom-call | flops 15703474176 | bytes 29097984 | tf_op jit(solution)/shard_map/cond/branch_0_fun/tiles/pallas_call | solution.py:227
  (89 shorter events, 4.5 us)
Async XLA Ops:
  1.5 1.5 collective-permute-start.37
  2.1 58.2 %copy-start.24 = (s32[4,512]{1,0:T(4,128)S(1)}, s32[4,512]{1,0:T(4,128)}, u32[]{:S(2)}) copy-start(s32[4,512]{1,0:T(4,128)} %param.22) | copy-start | bytes 24580
  2.1 58.2 %copy-start.25 = (s32[4]{0:T(128)S(1)}, s32[4]{0:T(128)}, u32[]{:S(2)}) copy-start(s32[4]{0:T(128)} %param.21) | copy-start | bytes 52
  2.1 62.3 %copy-start.18 = (bf16[512,3072]{1,0:T(8,128)(2,1)S(1)}, bf16[512,3072]{1,0:T(8,128)(2,1)}, u32[]{:S(2)}) copy-start(bf16[512,3072]{1,0:T(8,128)(2,1)} %param.19) | copy-start | bytes 9437188
  4.0 7.9 %collective-permute-start.38 = (bf16[512,128]{1,0:T(8,128)(2,1)S(1)}, bf16[512,128]{1,0:T(8,128)(2,1)S(1)}, u32[]{:S(2)}, u32[]{:S(2)}) collective-permute-start(bf16[512,128]{1,0:T(8,128)(2,1)S(1)} %broadcast_select_fusion), channel_id=1, source_target_pairs={{0,2},{1,3},{2,4},{3,5},{4,6},{5,7},{8,10},{9,11},{10,12},{11,13},... | collective-permute-start | bytes 393224 | tf_op jit(solution)/shard_map/ppermute | solution.py:363
  11.9 11.0 %collective-permute-start.39 = (bf16[512,128]{1,0:T(8,128)(2,1)S(1)}, bf16[512,128]{1,0:T(8,128)(2,1)S(1)}, u32[]{:S(2)}, u32[]{:S(2)}) collective-permute-start(bf16[512,128]{1,0:T(8,128)(2,1)S(1)} %broadcast_select_fusion.1), channel_id=1, source_target_pairs={{0,2},{1,3},{2,4},{3,5},{4,6},{5,7},{8,10},{9,11},{10,12},{11,13},... | collective-permute-start | bytes 393224 | tf_op jit(solution)/shard_map/ppermute | solution.py:363
  19.4 44.4 %collective-permute-start.34 = (bf16[512,768]{1,0:T(8,128)(2,1)}, bf16[512,768]{1,0:T(8,128)(2,1)}, u32[]{:S(2)}, u32[]{:S(2)}) collective-permute-start(bf16[512,768]{1,0:T(8,128)(2,1)} %get-tuple-element.248), channel_id=1, source_target_pairs={{0,8},{8,0},{16,24},{24,16},{1,9},{9,1},{17,25},{25,17},{2,10},{10... | collective-permute-start | bytes 2359304 | tf_op jit(solution)/shard_map/ppermute | solution.py:356
  20.9 42.9 %collective-permute-start.35 = (bf16[512,768]{1,0:T(8,128)(2,1)}, bf16[512,768]{1,0:T(8,128)(2,1)}, u32[]{:S(2)}, u32[]{:S(2)}) collective-permute-start(bf16[512,768]{1,0:T(8,128)(2,1)} %get-tuple-element.247), channel_id=1, source_target_pairs={{0,16},{8,24},{16,0},{24,8},{1,17},{9,25},{17,1},{25,9},{2,18},{10... | collective-permute-start | bytes 2359304 | tf_op jit(solution)/shard_map/ppermute | solution.py:356
  22.4 41.4 %collective-permute-start.36 = (bf16[512,768]{1,0:T(8,128)(2,1)}, bf16[512,768]{1,0:T(8,128)(2,1)}, u32[]{:S(2)}, u32[]{:S(2)}) collective-permute-start(bf16[512,768]{1,0:T(8,128)(2,1)} %get-tuple-element.246), channel_id=1, source_target_pairs={{0,24},{8,16},{16,8},{24,0},{1,25},{9,17},{17,9},{25,1},{2,26},{10... | collective-permute-start | bytes 2359304 | tf_op jit(solution)/shard_map/ppermute | solution.py:356
  22.9 6.0 %collective-permute-start.40 = (bf16[512,128]{1,0:T(8,128)(2,1)S(1)}, bf16[512,128]{1,0:T(8,128)(2,1)S(1)}, u32[]{:S(2)}, u32[]{:S(2)}) collective-permute-start(bf16[512,128]{1,0:T(8,128)(2,1)S(1)} %broadcast_select_fusion.2), channel_id=1, source_target_pairs={{0,2},{1,3},{2,4},{3,5},{4,6},{5,7},{8,10},{9,11},{10,12},{11,13},... | collective-permute-start | bytes 393224 | tf_op jit(solution)/shard_map/ppermute | solution.py:363
  28.9 28.9 %collective-permute-start.41 = (bf16[512,128]{1,0:T(8,128)(2,1)S(1)}, bf16[512,128]{1,0:T(8,128)(2,1)S(1)}, u32[]{:S(2)}, u32[]{:S(2)}) collective-permute-start(bf16[512,128]{1,0:T(8,128)(2,1)S(1)} %broadcast_select_fusion.3), channel_id=1, source_target_pairs={{0,8},{8,0},{16,24},{24,16},{1,9},{9,1},{17,25},{25,17},{2,10},{10... | collective-permute-start | bytes 393224 | tf_op jit(solution)/shard_map/ppermute | solution.py:356
  30.5 31.0 %collective-permute-start.42 = (bf16[512,128]{1,0:T(8,128)(2,1)S(1)}, bf16[512,128]{1,0:T(8,128)(2,1)S(1)}, u32[]{:S(2)}, u32[]{:S(2)}) collective-permute-start(bf16[512,128]{1,0:T(8,128)(2,1)S(1)} %broadcast_select_fusion.3), channel_id=1, source_target_pairs={{0,16},{8,24},{16,0},{24,8},{1,17},{9,25},{17,1},{25,9},{2,18},{10... | collective-permute-start | bytes 393224 | tf_op jit(solution)/shard_map/ppermute | solution.py:356
  57.8 6.0 %collective-permute-start.43 = (bf16[512,128]{1,0:T(8,128)(2,1)S(1)}, bf16[512,128]{1,0:T(8,128)(2,1)}, u32[]{:S(2)}, u32[]{:S(2)}) collective-permute-start(bf16[512,128]{1,0:T(8,128)(2,1)S(1)} %broadcast_select_fusion.3), channel_id=1, source_target_pairs={{0,24},{8,16},{16,8},{24,0},{1,25},{9,17},{17,9},{25,1},{2,26},{10... | collective-permute-start | bytes 393224 | tf_op jit(solution)/shard_map/ppermute | solution.py:356
  64.4 0.6 copy-start.22
  68.3 6.0 %copy-start.26 = (s32[4]{0:T(128)S(1)}, s32[4]{0:T(128)}, u32[]{:S(2)}) copy-start(s32[4]{0:T(128)} %get-tuple-element.163) | copy-start | bytes 52 | tf_op jit(solution)/shard_map/cond
  74.8 60.7 %slice-start = ((s8[4980736]{0:T(1024)(128)(4,1)}), s8[4194304]{0:T(1024)(128)(4,1)S(1)}, s32[]{:S(2)}) async-start(s8[4980736]{0:T(1024)(128)(4,1)} %bitcast.38), calls=%async_computation | async-start | bytes 8388608 | tf_op jit(solution)/shard_map/cond
  74.8 60.7 %slice-start.1 = ((s8[4980736]{0:T(1024)(128)(4,1)}), s8[786432]{0:T(1024)(128)(4,1)S(1)}, s32[]{:S(2)}) async-start(s8[4980736]{0:T(1024)(128)(4,1)} %bitcast.38), calls=%async_computation.1 | async-start | bytes 1572864 | tf_op jit(solution)/shard_map/cond
  83.2 41.8 %collective-permute-start.5 = (bf16[1216,768]{1,0:T(8,128)(2,1)}, bf16[1216,768]{1,0:T(8,128)(2,1)S(1)}, u32[]{:S(2)}, u32[]{:S(2)}) collective-permute-start(bf16[1216,768]{1,0:T(8,128)(2,1)} %whiten.4.refs_0_), channel_id=1, source_target_pairs={{2,0},{3,1},{4,2},{5,3},{6,4},{7,5},{10,8},{11,9},{12,10},{13,11},... | collective-permute-start | bytes 5603336 | tf_op jit(solution)/shard_map/cond/branch_0_fun/ppermute | solution.py:363
  84.5 41.8 %collective-permute-start = (bf16[1216,768]{1,0:T(8,128)(2,1)}, bf16[1216,768]{1,0:T(8,128)(2,1)}, u32[]{:S(2)}, u32[]{:S(2)}) collective-permute-start(bf16[1216,768]{1,0:T(8,128)(2,1)} %whiten.4.refs_0_), channel_id=1, source_target_pairs={{0,2},{1,3},{2,4},{3,5},{4,6},{5,7},{8,10},{9,11},{10,12},{11,13},... | collective-permute-start | bytes 5603336 | tf_op jit(solution)/shard_map/cond/branch_0_fun/ppermute | solution.py:363
  90.3 41.9 %collective-permute-start.10 = (bf16[1216,768]{1,0:T(8,128)(2,1)}, bf16[1216,768]{1,0:T(8,128)(2,1)S(1)}, u32[]{:S(2)}, u32[]{:S(2)}) collective-permute-start(bf16[1216,768]{1,0:T(8,128)(2,1)} %whiten.4.refs_0_), channel_id=1, source_target_pairs={{0,16},{8,24},{16,0},{24,8},{1,17},{9,25},{17,1},{25,9},{2,18},{10... | collective-permute-start | bytes 5603336 | tf_op jit(solution)/shard_map/cond/branch_0_fun/ppermute | solution.py:356
  91.9 42.0 %collective-permute-start.12 = (bf16[1216,768]{1,0:T(8,128)(2,1)}, bf16[1216,768]{1,0:T(8,128)(2,1)S(1)}, u32[]{:S(2)}, u32[]{:S(2)}) collective-permute-start(bf16[1216,768]{1,0:T(8,128)(2,1)} %whiten.4.refs_0_), channel_id=1, source_target_pairs={{0,8},{8,0},{16,24},{24,16},{1,9},{9,1},{17,25},{25,17},{2,10},{10... | collective-permute-start | bytes 5603336 | tf_op jit(solution)/shard_map/cond/branch_0_fun/ppermute | solution.py:356
  125.0 40.8 %collective-permute-start.6 = (bf16[1216,768]{1,0:T(8,128)(2,1)S(1)}, bf16[1216,768]{1,0:T(8,128)(2,1)}, u32[]{:S(2)}, u32[]{:S(2)}) collective-permute-start(bf16[1216,768]{1,0:T(8,128)(2,1)S(1)} %collective-permute-done.5.refs_2_), channel_id=1, source_target_pairs={{2,0},{3,1},{4,2},{5,3},{6,4},{7,5},{10,8},{11,9},{12,10},{13,11},... | collective-permute-start | bytes 5603336 | tf_op jit(solution)/shard_map/cond/branch_0_fun/ppermute | solution.py:363
  126.3 40.9 %collective-permute-start.1 = (bf16[1216,768]{1,0:T(8,128)(2,1)}, bf16[1216,768]{1,0:T(8,128)(2,1)}, u32[]{:S(2)}, u32[]{:S(2)}) collective-permute-start(bf16[1216,768]{1,0:T(8,128)(2,1)} %collective-permute-done.refs_0_), channel_id=1, source_target_pairs={{0,2},{1,3},{2,4},{3,5},{4,6},{5,7},{8,10},{9,11},{10,12},{11,13},... | collective-permute-start | bytes 5603336 | tf_op jit(solution)/shard_map/cond/branch_0_fun/ppermute | solution.py:363
  132.2 6.6 %copy-start.4 = (bf16[1216,768]{1,0:T(8,128)(2,1)}, bf16[1216,768]{1,0:T(8,128)(2,1)S(1)}, u32[]{:S(2)}) copy-start(bf16[1216,768]{1,0:T(8,128)(2,1)S(1)} %collective-permute-done.10.refs_0_) | copy-start | bytes 5603332 | tf_op jit(solution)/shard_map/cond
  132.3 18.7 %collective-permute-start.11 = (bf16[608,768]{1,0:T(8,128)(2,1)S(1)}, bf16[608,768]{1,0:T(8,128)(2,1)S(1)}, u32[]{:S(2)}, u32[]{:S(2)}) collective-permute-start(bf16[608,768]{1,0:T(8,128)(2,1)S(1)} %slice.38), channel_id=1, source_target_pairs={{0,8},{8,0},{16,24},{24,16},{1,9},{9,1},{17,25},{25,17},{2,10},{10... | collective-permute-start | bytes 2801672 | tf_op jit(solution)/shard_map/cond/branch_0_fun/ppermute | solution.py:356
  133.9 5.0 %copy-start.6 = (bf16[1216,768]{1,0:T(8,128)(2,1)}, bf16[1216,768]{1,0:T(8,128)(2,1)S(1)}, u32[]{:S(2)}) copy-start(bf16[1216,768]{1,0:T(8,128)(2,1)S(1)} %collective-permute-done.12.refs_0_) | copy-start | bytes 5603332 | tf_op jit(solution)/shard_map/cond
  133.9 18.0 %collective-permute-start.13 = (bf16[608,768]{1,0:T(8,128)(2,1)S(1)}, bf16[608,768]{1,0:T(8,128)(2,1)S(1)}, u32[]{:S(2)}, u32[]{:S(2)}) collective-permute-start(bf16[608,768]{1,0:T(8,128)(2,1)S(1)} %slice.39), channel_id=1, source_target_pairs={{0,16},{8,24},{16,0},{24,8},{1,17},{9,25},{17,1},{25,9},{2,18},{10... | collective-permute-start | bytes 2801672 | tf_op jit(solution)/shard_map/cond/branch_0_fun/ppermute | solution.py:356
  135.5 75.3 %collective-permute-start.16 = (bf16[1216,768]{1,0:T(8,128)(2,1)}, bf16[1216,768]{1,0:T(8,128)(2,1)}, u32[]{:S(2)}, u32[]{:S(2)}) collective-permute-start(bf16[1216,768]{1,0:T(8,128)(2,1)} %whiten.4.refs_0_), channel_id=1, source_target_pairs={{0,1},{1,0},{2,3},{3,2},{4,5},{5,4},{6,7},{7,6},{8,9},{9,8},{10,11... | collective-permute-start | bytes 5603336 | tf_op jit(solution)/shard_map/cond/branch_0_fun/ppermute | solution.py:359
  151.0 39.4 %copy-start.12 = (bf16[608,768]{1,0:T(8,128)(2,1)}, bf16[608,768]{1,0:T(8,128)(2,1)S(1)}, u32[]{:S(2)}) copy-start(bf16[608,768]{1,0:T(8,128)(2,1)S(1)} %collective-permute-done.11.refs_0_) | copy-start | bytes 2801668 | tf_op jit(solution)/shard_map/cond
  151.0 59.9 %collective-permute-start.14 = (bf16[1216,768]{1,0:T(8,128)(2,1)S(1)}, bf16[1216,768]{1,0:T(8,128)(2,1)}, u32[]{:S(2)}, u32[]{:S(2)}) collective-permute-start(bf16[1216,768]{1,0:T(8,128)(2,1)S(1)} %collective-permute-done.5.refs_2_), channel_id=1, source_target_pairs={{0,1},{1,0},{2,3},{3,2},{4,5},{5,4},{6,7},{7,6},{8,9},{9,8},{10,11... | collective-permute-start | bytes 5603336 | tf_op jit(solution)/shard_map/cond/branch_0_fun/ppermute | solution.py:359
  151.9 0.9 copy-start.14
  152.9 86.9 %collective-permute-start.15 = (bf16[1216,768]{1,0:T(8,128)(2,1)}, bf16[1216,768]{1,0:T(8,128)(2,1)}, u32[]{:S(2)}, u32[]{:S(2)}) collective-permute-start(bf16[1216,768]{1,0:T(8,128)(2,1)} %collective-permute-done.refs_0_), channel_id=1, source_target_pairs={{0,1},{1,0},{2,3},{3,2},{4,5},{5,4},{6,7},{7,6},{8,9},{9,8},{10,11... | collective-permute-start | bytes 5603336 | tf_op jit(solution)/shard_map/cond/branch_0_fun/ppermute | solution.py:359
  165.8 73.4 %collective-permute-start.8 = (bf16[1216,768]{1,0:T(8,128)(2,1)}, bf16[1216,768]{1,0:T(8,128)(2,1)}, u32[]{:S(2)}, u32[]{:S(2)}) collective-permute-start(bf16[1216,768]{1,0:T(8,128)(2,1)} %collective-permute-done.6.refs_4_), channel_id=1, source_target_pairs={{2,0},{3,1},{4,2},{5,3},{6,4},{7,5},{10,8},{11,9},{12,10},{13,11},... | collective-permute-start | bytes 5603336 | tf_op jit(solution)/shard_map/cond/branch_0_fun/ppermute | solution.py:363
  167.3 72.1 %collective-permute-start.3 = (bf16[1216,768]{1,0:T(8,128)(2,1)}, bf16[1216,768]{1,0:T(8,128)(2,1)}, u32[]{:S(2)}, u32[]{:S(2)}) collective-permute-start(bf16[1216,768]{1,0:T(8,128)(2,1)} %collective-permute-done.1.refs_0_), channel_id=1, source_target_pairs={{0,2},{1,3},{2,4},{3,5},{4,6},{5,7},{8,10},{9,11},{10,12},{11,13},... | collective-permute-start | bytes 5603336 | tf_op jit(solution)/shard_map/cond/branch_0_fun/ppermute | solution.py:363
  173.5 17.8 %copy-start.36 = (s32[4]{0:T(128)S(1)}, s32[4]{0:T(128)}, u32[]{:S(2)}) copy-start(s32[4]{0:T(128)} %constant.104.clone.1) | copy-start | bytes 52 | tf_op jit(solution)/shard_map/cond
  173.5 18.4 %copy-start.34 = (s32[4]{0:T(128)S(1)}, s32[4]{0:T(128)}, u32[]{:S(2)}) copy-start(s32[4]{0:T(128)} %constant.105.clone.1) | copy-start | bytes 52 | tf_op jit(solution)/shard_map/cond
  173.5 19.0 %copy-start.32 = (s32[4]{0:T(128)S(1)}, s32[4]{0:T(128)}, u32[]{:S(2)}) copy-start(s32[4]{0:T(128)} %constant.106.clone.1) | copy-start | bytes 52 | tf_op jit(solution)/shard_map/cond
  173.5 19.7 %copy-start.30 = (s32[4]{0:T(128)S(1)}, s32[4]{0:T(128)}, u32[]{:S(2)}) copy-start(s32[4]{0:T(128)} %constant.107.clone.1) | copy-start | bytes 52 | tf_op jit(solution)/shard_map/cond
  173.5 20.3 %copy-start.29 = (s32[4]{0:T(128)S(1)}, s32[4]{0:T(128)}, u32[]{:S(2)}) copy-start(s32[4]{0:T(128)} %constant.108.clone.1) | copy-start | bytes 52 | tf_op jit(solution)/shard_map/cond
  173.6 21.0 %copy-start.28 = (s32[4]{0:T(128)S(1)}, s32[4]{0:T(128)}, u32[]{:S(2)}) copy-start(s32[4]{0:T(128)} %constant.109.clone.1) | copy-start | bytes 52 | tf_op jit(solution)/shard_map/cond
  199.3 4.1 %copy-start.7 = (bf16[1216,768]{1,0:T(8,128)(2,1)S(1)}, bf16[1216,768]{1,0:T(8,128)(2,1)}, u32[]{:S(2)}) copy-start(bf16[1216,768]{1,0:T(8,128)(2,1)} %copy-done.6) | copy-start | bytes 5603332 | tf_op jit(solution)/shard_map/cond
  203.4 2.4 copy-start.5
  205.8 2.5 copy-start.13
  205.8 2.5 copy-start.15
  210.8 55.4 %collective-permute-start.7 = (bf16[1216,768]{1,0:T(8,128)(2,1)}, bf16[1216,768]{1,0:T(8,128)(2,1)S(1)}, u32[]{:S(2)}, u32[]{:S(2)}) collective-permute-start(bf16[1216,768]{1,0:T(8,128)(2,1)} %collective-permute-done.6.refs_4_), channel_id=1, source_target_pairs={{0,1},{1,0},{2,3},{3,2},{4,5},{5,4},{6,7},{7,6},{8,9},{9,8},{10,11... | collective-permute-start | bytes 5603336 | tf_op jit(solution)/shard_map/cond/branch_0_fun/ppermute | solution.py:359
  210.8 55.4 %collective-permute-start.2 = (bf16[1216,768]{1,0:T(8,128)(2,1)}, bf16[1216,768]{1,0:T(8,128)(2,1)S(1)}, u32[]{:S(2)}, u32[]{:S(2)}) collective-permute-start(bf16[1216,768]{1,0:T(8,128)(2,1)} %collective-permute-done.1.refs_0_), channel_id=1, source_target_pairs={{0,1},{1,0},{2,3},{3,2},{4,5},{5,4},{6,7},{7,6},{8,9},{9,8},{10,11... | collective-permute-start | bytes 5603336 | tf_op jit(solution)/shard_map/cond/branch_0_fun/ppermute | solution.py:359
  239.2 56.3 %collective-permute-start.9 = (bf16[1216,768]{1,0:T(8,128)(2,1)}, bf16[1216,768]{1,0:T(8,128)(2,1)S(1)}, u32[]{:S(2)}, u32[]{:S(2)}) collective-permute-start(bf16[1216,768]{1,0:T(8,128)(2,1)} %collective-permute-done.8.refs_6_), channel_id=1, source_target_pairs={{0,1},{1,0},{2,3},{3,2},{4,5},{5,4},{6,7},{7,6},{8,9},{9,8},{10,11... | collective-permute-start | bytes 5603336 | tf_op jit(solution)/shard_map/cond/branch_0_fun/ppermute | solution.py:359
  239.3 56.2 %collective-permute-start.4 = (bf16[1216,768]{1,0:T(8,128)(2,1)}, bf16[1216,768]{1,0:T(8,128)(2,1)S(1)}, u32[]{:S(2)}, u32[]{:S(2)}) collective-permute-start(bf16[1216,768]{1,0:T(8,128)(2,1)} %collective-permute-done.3.refs_2_), channel_id=1, source_target_pairs={{0,1},{1,0},{2,3},{3,2},{4,5},{5,4},{6,7},{7,6},{8,9},{9,8},{10,11... | collective-permute-start | bytes 5603336 | tf_op jit(solution)/shard_map/cond/branch_0_fun/ppermute | solution.py:359
  266.2 1.3 copy-start.17
  295.5 1.2 copy-start.20
  295.5 1.8 copy-start.21
